TPU v7x, 256 devices: a whole 4x4x8 slice. The times are simulated.
256 devices in a mesh: row: 32 (over z_hi, y, core), col: 8 (over z_lo, x).
Axes of the slice: x: 4, y: 4, z: 8 (z_hi: 4, z_lo: 2; z = z_hi * 2 + z_lo), core: 2. Of those that a mesh axis runs over, the one named last changes fastest.
Arguments:
- kernel: float32 [4, 32, 128, 16, 8, 128], P(None, 'row', None, None, 'col'), may hold values from 0 to 20
Outputs:
- factored: float32 [4, 32, 128, 16, 8, 128], P(None, 'row', None, None, 'col')
All inputs are finite; a program needn't handle non-finite values.
Results may differ from a plain program's by a relative error of at most 0.00006.
Values sent between devices are 32-bit elements; how exact they have to be, the bound alone decides.
No kernel may reach another device: no remote copies, remote signals or barrier semaphores. Data moves between devices by JAX's collectives and lax.ppermute only.
A program may use at most 64 MiB of HBM per device.

v0:
```python
import jax
import jax.numpy as jnp
from jax import lax
from jax.sharding import PartitionSpec as P


def from_root(value, axis, source):
    kept = jnp.where(lax.axis_index(axis) == source, value, 0).astype(value.dtype)
    return lax.psum(kept, axis)


def local(kernel):
    row_count = kernel.shape[0]
    block_width = kernel.shape[2]
    col_count = kernel.shape[3]
    local_block = kernel.reshape(row_count * block_width, col_count * block_width)
    row_pos = lax.axis_index("row")
    col_pos = lax.axis_index("col")
    first_cols = local_block[:, :block_width]
    first_rows = local_block[:block_width, :]
    gathered = lax.all_gather(first_cols, "col", axis=1, tiled=True)
    panel_cols = gathered[:, : 2 * block_width]
    row_pieces = []
    for source in range(2):
        row_pieces.append(from_root(first_rows, "row", source))
    panel_rows = jnp.concatenate(row_pieces, 0)
    diag_wide = lax.all_gather(panel_rows[:, :block_width], "col", axis=1, tiled=True)
    diag_block = diag_wide[:, : 2 * block_width]
    factor = jnp.linalg.cholesky(diag_block)
    left_solved = lax.linalg.triangular_solve(factor, panel_cols.T, left_side=True, lower=True).T
    top_solved = lax.linalg.triangular_solve(factor, panel_rows, left_side=True, lower=True)
    updated = local_block - jnp.dot(left_solved, top_solved, precision=lax.Precision.HIGHEST)
    row_sel = jnp.minimum(row_pos, 1) * block_width
    col_sel = jnp.minimum(col_pos, 1) * block_width
    top_piece = lax.dynamic_slice_in_dim(top_solved, row_sel, block_width, 0)
    updated = updated.at[:block_width, :].set(
        jnp.where(row_pos < 2, top_piece, updated[:block_width, :])
    )
    left_piece = lax.dynamic_slice_in_dim(left_solved, col_sel, block_width, 1)
    updated = updated.at[:, :block_width].set(
        jnp.where(col_pos < 2, left_piece, updated[:, :block_width])
    )
    corner = lax.dynamic_slice(factor, (row_sel, col_sel), (block_width, block_width))
    corner_new = jnp.where(
        (row_pos < 2) & (col_pos < 2), corner, updated[:block_width, :block_width]
    )
    updated = updated.at[:block_width, :block_width].set(corner_new)
    return updated.reshape(kernel.shape)


def solution(mesh):
    placed = (P(None, "row", None, None, "col", None),)
    return jax.shard_map(
        local,
        mesh=mesh,
        in_specs=placed,
        out_specs=P(None, "row", None, None, "col", None),
        check_vma=False,
    )
```

profile of v0, /device:TPU:1, one launch (start us, length us, event | category | flops | bytes accessed | tf_op | source)
XLA Modules:
  0.0 436.9 jit_solution(16994595981871551114)
XLA Ops:
  7.4 2.7 broadcast_select_fusion.1
  10.0 2.0 copy.2
  12.1 2.0 copy.3
  14.0 0.0 all-reduce.4.cloned.1.call-update
  14.0 0.0 all-gather.5.cloned.1.call-start
  14.1 4.1 copy.14
  18.2 0.7 slice.153
  19.0 0.0 all-gather.5.cloned.1.call-update
  19.0 0.2 all-gather.3.cloned.1.call-start
  19.2 295.3 %all-reduce.4.cloned.1.call-done = (f32[128,2048]{0,1:T(8,128)}, f32[128,2048]{0,1:T(8,128)}) async-done(((f32[128,2048]{0,1:T(8,128)}, f32[128,2048]{0,1:T(8,128)}), (f32[128,2048]{0,1:T(8,128)}, f32[128,2048]{0,1:T(8,128)})) %all-reduce.4.cloned.1.call-update) | async-done | bytes 2097168 | tf_op jit(solution)/shard_map/psum | solution.py:9
  314.6 1.5 pad_maximum_fusion.4
  316.1 0.0 all-gather.3.cloned.1.call-update
  316.2 0.6 compare_reduce_fusion
  316.8 1.1 slice_bitcast_fusion
  317.9 33.6 %all-gather.3.cloned.1.call-done = f32[256,1024]{0,1:T(8,128)} async-done(((f32[256,128]{0,1:T(8,128)}), f32[256,1024]{0,1:T(8,128)}) %all-gather.3.cloned.1.call-update) | async-done | bytes 1048592 | tf_op jit(solution)/shard_map/all_gather | solution.py:27
  351.4 1.0 slice.152
  352.4 0.1 copy.4
  352.5 0.0 copy-start.1
  352.5 1.1 fusion.7
  353.6 11.7 %cholesky.50 = f32[128,128]{1,0:T(8,128)S(1)} custom-call(f32[128,128]{1,0:T(8,128)S(1)} %cholesky.118), custom_call_target="Cholesky" | custom-call | tf_op jit(solution)/shard_map/jit(cholesky)/cholesky | solution.py:29
  365.4 9.8 %custom-call.16 = f32[1,128,128]{1,2,0:T(8,128)S(1)} custom-call(f32[1,128,128]{2,1,0:T(8,128)S(1)} %get-tuple-element.68), custom_call_target="InvertDiagBlocksLowerTriangular" | custom-call | tf_op jit(solution)/shard_map/jit(cholesky)/cholesky | solution.py:29
  375.2 0.2 constant_dynamic-update-slice_fusion.1
  375.4 0.3 convolution_subtract_fusion.3
  375.7 11.7 %cholesky.105 = f32[128,128]{1,0:T(8,128)S(1)} custom-call(f32[128,128]{1,0:T(8,128)S(1)} %convolution_subtract_fusion.3), custom_call_target="Cholesky" | custom-call | tf_op jit(solution)/shard_map/jit(cholesky)/cholesky | solution.py:29
  387.5 0.7 compare_reduce_fusion.1
  389.5 0.7 fusion.8
  390.2 0.1 triangular_solve.68
  390.3 4.1 while.4
  390.3 0.7 fusion.28
  391.0 1.4 bitcast_dynamic-update-slice_fusion.2
  392.4 0.6 fusion.28
  393.0 1.4 bitcast_dynamic-update-slice_fusion.2
  394.4 19.9 %custom-call.17 = f32[2,128,128]{1,2,0:T(8,128)S(1)} custom-call(f32[2,128,128]{2,1,0:T(8,128)S(1)} %get-tuple-element.48), custom_call_target="InvertDiagBlocksLowerTriangular" | custom-call | tf_op jit(solution)/shard_map/triangular_solve | solution.py:30
  414.3 0.4 fusion.5
  414.7 0.6 convolution_subtract_fusion.2
  415.3 0.1 copy.5
  415.5 0.0 copy-done.2
  415.5 0.0 copy-start
  415.5 1.1 fusion.13
  416.6 0.4 fusion.15
  416.9 0.0 copy-done.1
  417.0 1.8 convolution_subtract_fusion.1
  418.8 1.1 fusion.14
  419.9 4.7 %convolution_subtract_fusion = f32[512,2048]{1,0:T(8,128)S(1)} fusion(f32[128,2048]{1,0:T(8,128)S(1)} %fusion.14, f32[128,2048]{1,0:T(8,128)S(1)} %fusion.13, f32[128,512]{0,1:T(8,128)S(1)} %fusion.15, f32[128,512]{0,1:T(8,128)S(1)} %copy.5, f32[64,8,16,128]{3,2,1,0:T(8,128)S(1)} %bitcast.61), kind=kOutput, calls=%fused_computation.3 | convolution fusion | flops 3222929408 | bytes 11010048 | tf_op jit(solution)/shard_map/dot_general | solution.py:32
  424.6 0.5 fusion.2
  425.0 0.6 select_select_fusion
  425.7 0.9 fusion.9
  426.5 2.9 copy.10
  (13 shorter events, 0.1 us)
Async XLA Ops:
  7.4 307.2 %all-reduce.4.cloned.1.call-start = ((), (), s32[]{:S(2)}) async-start(), calls=%async_computation.2 | async-start | bytes 4194304 | tf_op jit(solution)/shard_map/psum | solution.py:9
  14.0 302.8 %all-gather.5.cloned.1.call-start = ((), (), s32[]{:S(2)}) async-start(), calls=%async_computation.1 | async-start | bytes 2359296 | tf_op jit(solution)/shard_map/all_gather | solution.py:21
  19.0 332.4 %all-gather.3.cloned.1.call-start = ((), (), s32[]{:S(2)}) async-start(), calls=%async_computation | async-start | bytes 1179648 | tf_op jit(solution)/shard_map/all_gather | solution.py:27
  316.1 99.4 %copy-start.2 = (f32[128,2048]{0,1:T(8,128)S(1)}, f32[128,2048]{0,1:T(8,128)}, u32[]{:S(2)}) copy-start(f32[128,2048]{0,1:T(8,128)} %get-tuple-element.58) | copy-start | bytes 3145732
  352.5 64.4 %copy-start.1 = (f32[128,2048]{0,1:T(8,128)S(1)}, f32[128,2048]{0,1:T(8,128)}, u32[]{:S(2)}) copy-start(f32[128,2048]{0,1:T(8,128)} %get-tuple-element.57) | copy-start | bytes 3145732
  415.5 4.4 %copy-start = (f32[4,1,128,16,1,128]{5,4,3,2,1,0:T(1,128)S(1)}, f32[4,1,128,16,1,128]{5,4,3,2,1,0:T(1,128)}, u32[]{:S(2)}) copy-start(f32[4,1,128,16,1,128]{5,4,3,2,1,0:T(1,128)} %param.7) | copy-start | bytes 12582916
Sparse Core Ops, SparseCore 0:
  14.2 300.3 all-reduce.3
Sparse Core Ops, SparseCore 1:
  19.1 47.7 all-gather.4
  316.2 35.2 all-gather.2
where the time goes:
time: 442 us; the launch traced here: 437 us
  waiting for transfers between devices  329 us (74%)
  other arithmetic  62.5 us (14%)
  local copies, waits for them, and re-layouts  18.3 us (4%)
  between operations  16.4 us (4%)
  matrix products  10.5 us (2%)
    psum x1, waiting for transfers between devices, from_root(): return lax.psum(kept, axis)  295 us
    another operation x6, other arithmetic, local(): factor = jnp.linalg.cholesky(diag_block)  34 us
    all_gather x1, waiting for transfers between devices, local(): lax.all_gather(panel_rows[:, :block_width], 'col', axis=1, tiled=True)  33.6 us
    another operation x3, other arithmetic, local(): lax.linalg.triangular_solve(factor, panel_cols.T, left_side=True, lower=T...  20.6 us
  transfers between devices with their start and end apart: 3, of which 2 were waited for; matrix products, arithmetic and copies ran while one was open for 2% of the time, Pallas kernels for 0%

commit v1 on v0

v1 whole, which is shorter than its diff:
```python
import functools

import jax
import jax.numpy as jnp
from jax import lax
from jax.experimental import pallas as pl
from jax.experimental.pallas import tpu as pltpu
from jax.sharding import PartitionSpec as P

HIGHEST = lax.Precision.HIGHEST
BLK = 128
PANEL = 2 * BLK
AXES = ("row", "col")


def device_id(zh, y, core, zl, x):
    return ((zh % 4) * 8 + (y % 4) * 2 + core) * 8 + zl * 4 + x % 4


def all_places():
    for zh in range(4):
        for y in range(4):
            for core in range(2):
                for zl in range(2):
                    for x in range(4):
                        yield zh, y, core, zl, x


def send(value, target):
    pairs = []
    for place in all_places():
        to = target(*place)
        if to is not None:
            pairs.append((device_id(*place), device_id(*to)))
    return lax.ppermute(value, AXES, pairs)


def dot_nt(a, b):
    return lax.dot_general(
        a, b, (((1,), (1,)), ((), ())), precision=HIGHEST, preferred_element_type=jnp.float32
    )


def dot_tn(a, b):
    return lax.dot_general(
        a, b, (((0,), (0,)), ((), ())), precision=HIGHEST, preferred_element_type=jnp.float32
    )


def dot_nn(a, b):
    return lax.dot_general(
        a, b, (((1,), (0,)), ((), ())), precision=HIGHEST, preferred_element_type=jnp.float32
    )


def factor_kernel(nb, d00_ref, d01_ref, d11_ref, u_ref, w_ref, m_ref):
    lane = lax.broadcasted_iota(jnp.int32, (nb, BLK), 1)
    sub = lax.broadcasted_iota(jnp.int32, (nb, BLK), 0)
    for p in range(PANEL // nb):
        k0 = p * nb
        half = k0 // BLK
        c0 = k0 % BLK
        if half == 0:
            tiles = [d00_ref[k0 : k0 + nb, :], d01_ref[k0 : k0 + nb, :]]
        else:
            tiles = [None, d11_ref[c0 : c0 + nb, :]]
        for t in range(2):
            one = jnp.where(lane + t * BLK == sub + k0, 1.0, 0.0)
            tiles.append(one if t <= half else None)
        if p > 0:
            lhs = m_ref[0:k0, k0 : k0 + nb]
            for t in range(4):
                if tiles[t] is not None:
                    tiles[t] = tiles[t] - dot_tn(lhs, m_ref[0:k0, t * BLK : (t + 1) * BLK])
        spread = [
            jnp.broadcast_to(tiles[half][:, c0 + j : c0 + j + 1], (nb, BLK)) for j in range(nb)
        ]
        pivots = jnp.ones((nb, BLK), jnp.float32)
        for k in range(nb):
            column = spread[k]
            pivot = jnp.broadcast_to(column[k : k + 1, :], (nb, BLK))
            pivots = jnp.where(sub == k, pivot, pivots)
            if k < nb - 1:
                ratio = jnp.where(sub > k, column, 0.0) * (1.0 / pivot)
                for j in range(k + 1, nb):
                    spread[j] = spread[j] - ratio * jnp.broadcast_to(column[j : j + 1, :], (nb, BLK))
                for t in range(4):
                    if tiles[t] is not None:
                        tiles[t] = tiles[t] - ratio * jnp.broadcast_to(
                            tiles[t][k : k + 1, :], (nb, BLK)
                        )
        scale = lax.rsqrt(pivots)
        for t in range(4):
            if tiles[t] is None:
                out = jnp.zeros((nb, BLK), jnp.float32)
            else:
                out = tiles[t] * scale
                if t == half:
                    out = jnp.where(lane >= sub + c0, out, 0.0)
            m_ref[k0 : k0 + nb, t * BLK : (t + 1) * BLK] = out
    u_ref[...] = m_ref[:, :PANEL]
    w_ref[...] = m_ref[:, PANEL:]


def factorize(d00, d01, d11):
    square = jax.ShapeDtypeStruct((PANEL, PANEL), jnp.float32)
    vmem = pl.BlockSpec(memory_space=pltpu.VMEM)
    return pl.pallas_call(
        functools.partial(factor_kernel, 32),
        out_shape=[square, square],
        in_specs=[vmem] * 3,
        out_specs=[vmem] * 2,
        scratch_shapes=[pltpu.VMEM((PANEL, 2 * PANEL), jnp.float32)],
        compiler_params=pltpu.CompilerParams(vmem_limit_bytes=24 * 1024 * 1024),
        cost_estimate=pl.CostEstimate(flops=10000000, bytes_accessed=800000, transcendentals=0),
        name="factorize",
    )(d00, d01, d11)


def update_kernel(rows, pos_ref, a_ref, near_ref, far_ref, *refs):
    mine = refs[0:4]
    other = refs[4:8]
    wnear_ref, wfar_ref, wmine_ref, wother_ref, u_ref, o_ref, top_ref, left_ref = refs[8:]
    step = pl.program_id(0)
    row, col = pos_ref[0], pos_ref[1]
    y, zh = pos_ref[2], pos_ref[3]

    @pl.when(step == 0)
    def _():
        left_ref[...] = dot_nt(near_ref[...], wnear_ref[...]) + dot_nt(far_ref[...], wfar_ref[...])
        for d in range(4):
            top_ref[:, d * 512 : (d + 1) * 512] = dot_nt(wmine_ref[...], mine[d][...]) + dot_nt(
                wother_ref[...], other[d][...]
            )

    lhs = left_ref[pl.ds(pl.multiple_of(step * rows, rows), rows), :]
    for n in range(8):
        product = dot_nn(lhs, top_ref[:, n * 256 : (n + 1) * 256])
        for h in range(2):
            slot = 2 * n + h
            j = 4 * lax.rem(y + slot // 4, 4) + lax.rem(zh + slot % 4, 4)
            at = pl.ds(j, rows, 16)
            o_ref[at, :] = a_ref[at, :] - product[:, h * BLK : (h + 1) * BLK]

    @pl.when((row < 2) & (step == 0))
    def _():
        first = pl.ds(pl.multiple_of(row * BLK, BLK), BLK)
        for slot in range(16):
            j = 4 * lax.rem(y + slot // 4, 4) + lax.rem(zh + slot % 4, 4)
            o_ref[pl.ds(j, BLK, 16), :] = top_ref[first, slot * BLK : (slot + 1) * BLK]

    @pl.when(col < 2)
    def _():
        wide = left_ref[pl.ds(pl.multiple_of(step * rows, rows), rows), :]
        o_ref[pl.ds(0, rows, 16), :] = jnp.where(col == 0, wide[:, :BLK], wide[:, BLK:])

    @pl.when((row < 2) & (col < 2) & (step == 0))
    def _():
        strip = u_ref[pl.ds(pl.multiple_of(col * BLK, BLK), BLK), :]
        o_ref[pl.ds(0, BLK, 16), :] = jnp.where(row == 0, strip[:, :BLK], strip[:, BLK:]).T


def update(pos, a, near, far, mine, other, wnear, wfar, wmine, wother, upper):
    rows = BLK
    vmem = pl.BlockSpec(memory_space=pltpu.VMEM)
    tile = pl.BlockSpec((rows * 16, BLK), lambda i: (i, 0))
    return pl.pallas_call(
        functools.partial(update_kernel, rows),
        grid=(4,),
        out_shape=jax.ShapeDtypeStruct(a.shape, jnp.float32),
        in_specs=[pl.BlockSpec(memory_space=pltpu.SMEM), tile] + [vmem] * 15,
        out_specs=tile,
        scratch_shapes=[
            pltpu.VMEM((PANEL, 2048), jnp.float32),
            pltpu.VMEM((512, PANEL), jnp.float32),
        ],
        compiler_params=pltpu.CompilerParams(vmem_limit_bytes=40 * 1024 * 1024),
        cost_estimate=pl.CostEstimate(
            flops=5000000000, bytes_accessed=12000000, transcendentals=0
        ),
        name="update",
    )(pos, a, near, far, *mine, *other, wnear, wfar, wmine, wother, upper)


def local(kernel):
    row = lax.axis_index("row")
    col = lax.axis_index("col")
    zh, y, core = row // 8, (row // 2) % 4, row % 2
    x = col % 4
    flat = kernel.reshape(512 * 16, BLK)
    left = kernel.reshape(4, BLK, 16, BLK)[:, :, 0, :]

    with jax.named_scope("diag"):
        block = left[0]
        d00 = send(block, lambda zh, y, core, zl, x: (0, 0, 0, 0, 1) if (zh, y, core, zl, x) == (0, 0, 0, 0, 0) else None)
        d01 = send(block[64:], lambda zh, y, core, zl, x: (0, 0, 1, 0, 1) if (zh, y, core, zl, x) == (0, 0, 0, 0, 1) else None)
        packed = jnp.where(
            core == 0, jnp.concatenate([d00, block[:64]]), jnp.concatenate([d01, block])
        )
        packed = jnp.where((row < 2) & (col == 1), packed, 0.0)
        got = [
            send(packed, lambda zh, y, core, zl, x, s=s: (0, 0, core, 0, x + s) if (zh, y, zl, x) == (0, 0, 0, 1) else None)
            for s in (1, 3, 2)
        ]
        packed = packed + got[0] + got[1] + got[2]
        got = [
            send(packed, lambda zh, y, core, zl, x, s=s: (0, y + s, core, 0, x) if (zh, y, zl) == (0, 0, 0) else None)
            for s in (1, 3, 2)
        ]
        packed = packed + got[0] + got[1] + got[2]
        got = [
            send(packed, lambda zh, y, core, zl, x, s=s: (zh + s, y, core, 0, x) if (zh, zl) == (0, 0) else None)
            for s in (1, 3, 2)
        ]
        packed = packed + got[0] + got[1] + got[2]
        got = send(packed, lambda zh, y, core, zl, x: (zh, y, core, 1, x) if zl == 0 else None)
        packed = packed + got
        swapped = send(packed, lambda zh, y, core, zl, x: (zh, y, 1 - core, zl, x))
        first = jnp.where(core == 0, packed, swapped)
        second = jnp.where(core == 0, swapped, packed)
        upper, inverse = factorize(
            first[:128], jnp.concatenate([first[128:], second[:64]]), second[64:]
        )

    with jax.named_scope("rows"):
        r1 = send(left, lambda zh, y, core, zl, x: (zh, y, core, 0, 3 - x) if zl == 0 and x < 2 else None)
        r2 = send(left, lambda zh, y, core, zl, x: (zh, y, core, 1, x) if zl == 0 and x < 2 else None)
        r3 = send(r2, lambda zh, y, core, zl, x: (zh, y, core, 1, 3 - x) if zl == 1 and x < 2 else None)
        near = jnp.where(col < 2, left, 0.0) + r1 + r2 + r3
        far = send(near, lambda zh, y, core, zl, x: (zh, y, core, zl, x ^ 1))

    with jax.named_scope("cols"):
        piece = None
        for s in range(4):
            part = lax.dynamic_index_in_dim(left, (y + s) % 4, 0, keepdims=False)
            got = send(
                part,
                lambda zh, y, core, zl, x, s=s: (zh, y + s, x, y // 2, 2 * (y % 2) + core)
                if zl == 0 and x < 2
                else None,
            )
            piece = got if piece is None else piece + got
        over_z = [piece] + [
            send(piece, lambda zh, y, core, zl, x, s=s: (zh - s, y, core, zl, x)) for s in (1, 2, 3)
        ]
        own = jnp.concatenate([v[None] for v in over_z])
        up = send(own, lambda zh, y, core, zl, x: (zh, y - 1, core, zl, x))
        down = send(own, lambda zh, y, core, zl, x: (zh, y + 1, core, zl, x))
        opposite = jnp.concatenate(
            [
                send(down[:2], lambda zh, y, core, zl, x: (zh, y + 1, core, zl, x)),
                send(up[2:], lambda zh, y, core, zl, x: (zh, y - 1, core, zl, x)),
            ]
        )
        mine = [own, up, opposite, down]
        other = [send(v, lambda zh, y, core, zl, x: (zh, y, 1 - core, zl, x)) for v in mine]

    with jax.named_scope("final"):
        lo, hi = inverse[:, :BLK], inverse[:, BLK:]
        near_is_lo = (x == 0) | (x == 3)
        wnear, wfar = jnp.where(near_is_lo, lo, hi), jnp.where(near_is_lo, hi, lo)
        wmine, wother = jnp.where(core == 0, lo, hi), jnp.where(core == 0, hi, lo)
        pos = jnp.stack([row, col, y, zh]).astype(jnp.int32)
        tall = lambda v: v.reshape(512, BLK)
        out = update(
            pos, flat, tall(near), tall(far), [tall(v) for v in mine], [tall(v) for v in other],
            wnear, wfar, wmine, wother, upper,
        )
    return out.reshape(kernel.shape)


def solution(mesh):
    placed = P(None, "row", None, None, "col", None)
    return jax.shard_map(
        local, mesh=mesh, in_specs=(placed,), out_specs=placed, check_vma=False
    )
```

time: 442 us -> 88.4 us (0.20); the launches traced: 437 us -> 87.9 us
  waiting for transfers between devices: 329 us -> 7.33 us
  other arithmetic: 62.5 us -> 1.31 us
  starting transfers between devices: 0.27 us -> 51.6 us
  Pallas kernels: 0 us -> 22.7 us
  between operations: 16.4 us -> 0.68 us
  local copies, waits for them, and re-layouts: 18.3 us -> 4.25 us
  matrix products: 10.5 us -> 0 us
    psum x1 -> x0, waiting for transfers between devices: 295 us -> none  [from_root(): return lax.psum(kept, axis)]
    another operation x11 -> x1, other arithmetic: 55.9 us -> 0.08 us  [local(): pos = jnp.stack([row, col, y, zh]).astype(jnp.int32)]
    ppermute x0 -> x32, starting transfers between devices: none -> 51.6 us  [send(): return lax.ppermute(value, AXES, pairs)]
    all_gather x2 -> x0, waiting for transfers between devices: 33.6 us -> none  [the longest x1 33.6 us: local(): lax.all_gather(panel_rows[:, :block_width], 'col', axis=1, tiled=True)]
    pallas_call x0 -> x2, Pallas kernels: none -> 22.7 us  [the longest x1 15 us: update(): pl.pallas_call(functools.partial(update_kernel, rows), grid=(4,), out_sha...]
    ppermute x0 -> x32, waiting for transfers between devices: none -> 7.33 us  [send(): return lax.ppermute(value, AXES, pairs)]
    another operation x8 -> x0, matrix products: 5.8 us -> none  [the longest x3 3.97 us: local(): lax.linalg.triangular_solve(factor, panel_rows, left_side=True, lower=True)]
    dot_general x1 -> x0, matrix products: 4.68 us -> none  [local(): jnp.dot(left_solved, top_solved, precision=lax.Precision.HIGHEST)]
  transfers between devices with their start and end apart: 3 -> 32, of which waited for: 2 -> 4; matrix products, arithmetic and copies ran while one was open for 2% -> 2% of each run, Pallas kernels for 0% -> 9%
where the time goes in v1:
time: 88.4 us; the launch traced here: 87.9 us
  starting transfers between devices  51.6 us (58%)
  Pallas kernels  22.7 us (26%)
  waiting for transfers between devices  7.33 us (8%)
  local copies, waits for them, and re-layouts  4.25 us (5%)
  other arithmetic  1.31 us (1%)
    ppermute x32, starting transfers between devices, send(): return lax.ppermute(value, AXES, pairs)  51.6 us
    pallas_call x1, Pallas kernels, update(): pl.pallas_call(functools.partial(update_kernel, rows), grid=(4,), out_sha...  15 us
    pallas_call x1, Pallas kernels, factorize(): pl.pallas_call(functools.partial(factor_kernel, 32), out_shape=[square, s...  7.71 us
    ppermute x32, waiting for transfers between devices, send(): return lax.ppermute(value, AXES, pairs)  7.33 us
    unnamed x6, local copies, waits for them, and re-layouts  4.12 us
  transfers between devices with their start and end apart: 32, of which 4 were waited for; matrix products, arithmetic and copies ran while one was open for 2% of the time, Pallas kernels for 9%

profile of v1, /device:TPU:1, one launch (start us, length us, event | category | flops | bytes accessed | tf_op | source)
XLA Modules:
  0.0 87.9 jit_solution(17865461089637313734)
XLA Ops:
  0.0 3.5 %copy.5 = f32[4,1,128,16,1,128]{5,2,3,0,4,1:T(8,128)S(1)} copy(f32[4,1,128,16,1,128]{5,4,3,2,1,0:T(1,128)} %param.1) | data formatting | bytes 8388608 | tf_op args[0]
  3.5 0.0 copy-start.1
  3.5 0.7 collective-permute-start.19
  4.2 0.7 collective-permute-start.20
  4.9 0.6 copy-done.1
  5.5 4.4 %collective-permute-start.1 = (f32[4,128,128]{2,1,0:T(8,128)S(1)}, f32[4,128,128]{2,1,0:T(8,128)S(1)}, u32[]{:S(2)}, u32[]{:S(2)}) collective-permute-start(f32[4,128,128]{2,1,0:T(8,128)S(1)} %get-tuple-element.12), channel_id=1, source_target_pairs={{0,4},{1,5},{8,12},{9,13},{16,20},{17,21},{24,28},{25,29},{32,36},... | collective-permute-start | bytes 786440 | tf_op jit(solution)/shard_map/rows/ppermute | solution.py:35
  10.1 0.0 collective-permute-done.19
  10.1 0.7 collective-permute-start.23
  10.8 1.3 %collective-permute-start.22 = (f32[192,128]{1,0:T(8,128)S(1)}, f32[192,128]{1,0:T(8,128)S(1)}, u32[]{:S(2)}, u32[]{:S(2)}) collective-permute-start(f32[192,128]{1,0:T(8,128)S(1)} %fusion), channel_id=1, source_target_pairs={{1,0},{9,8}} | collective-permute-start | bytes 294920 | tf_op jit(solution)/shard_map/diag/ppermute | solution.py:35
  12.1 0.7 collective-permute-start.21
  12.8 5.8 %collective-permute-start.7 = (f32[128,128]{1,0:T(8,128)S(1)}, f32[128,128]{1,0:T(8,128)S(1)}, u32[]{:S(2)}, u32[]{:S(2)}) collective-permute-start(f32[128,128]{1,0:T(8,128)S(1)} %get-tuple-element.20), channel_id=1, source_target_pairs={{0,48},{1,56},{8,49},{9,57},{16,2},{17,10},{24,3},{25,11},{32,20},... | collective-permute-start | bytes 196616 | tf_op jit(solution)/shard_map/cols/ppermute | solution.py:35
  18.6 0.0 copy-start
  18.6 1.9 %collective-permute-start.6 = (f32[128,128]{1,0:T(8,128)S(1)}, f32[128,128]{1,0:T(8,128)S(1)}, u32[]{:S(2)}, u32[]{:S(2)}) collective-permute-start(f32[128,128]{1,0:T(8,128)S(1)} %get-tuple-element.18), channel_id=1, source_target_pairs={{0,32},{1,40},{8,33},{9,41},{16,50},{17,58},{24,51},{25,59},{32,4}... | collective-permute-start | bytes 196616 | tf_op jit(solution)/shard_map/cols/ppermute | solution.py:35
  20.5 2.8 %collective-permute-start.4 = (f32[128,128]{1,0:T(8,128)S(1)}, f32[128,128]{1,0:T(8,128)S(1)}, u32[]{:S(2)}, u32[]{:S(2)}) collective-permute-start(f32[128,128]{1,0:T(8,128)S(1)} %get-tuple-element.19), channel_id=1, source_target_pairs={{0,0},{1,8},{8,1},{9,9},{16,18},{17,26},{24,19},{25,27},{32,36},{3... | collective-permute-start | bytes 196616 | tf_op jit(solution)/shard_map/cols/ppermute | solution.py:35
  23.3 0.0 collective-permute-done.21
  23.4 1.3 %collective-permute-start.5 = (f32[128,128]{1,0:T(8,128)S(1)}, f32[128,128]{1,0:T(8,128)S(1)}, u32[]{:S(2)}, u32[]{:S(2)}) collective-permute-start(f32[128,128]{1,0:T(8,128)S(1)} %get-tuple-element.17), channel_id=1, source_target_pairs={{0,16},{1,24},{8,17},{9,25},{16,34},{17,42},{24,35},{25,43},{32,52... | collective-permute-start | bytes 196616 | tf_op jit(solution)/shard_map/cols/ppermute | solution.py:35
  24.7 1.3 %collective-permute-start = (f32[4,128,128]{2,1,0:T(8,128)S(1)}, f32[4,128,128]{2,1,0:T(8,128)S(1)}, u32[]{:S(2)}, u32[]{:S(2)}) collective-permute-start(f32[4,128,128]{2,1,0:T(8,128)S(1)} %get-tuple-element.12), channel_id=1, source_target_pairs={{0,3},{1,2},{8,11},{9,10},{16,19},{17,18},{24,27},{25,26},{32,35},... | collective-permute-start | bytes 786440 | tf_op jit(solution)/shard_map/rows/ppermute | solution.py:35
  26.0 0.0 collective-permute-done.6
  26.0 1.9 %collective-permute-start.26 = (f32[192,128]{1,0:T(8,128)S(1)}, f32[192,128]{1,0:T(8,128)S(1)}, u32[]{:S(2)}, u32[]{:S(2)}) collective-permute-start(f32[192,128]{1,0:T(8,128)S(1)} %add_add_fusion.3), channel_id=1, source_target_pairs={{0,32},{1,33},{2,34},{3,35},{8,40},{9,41},{10,42},{11,43}} | collective-permute-start | bytes 294920 | tf_op jit(solution)/shard_map/diag/ppermute | solution.py:35
  27.9 1.3 %collective-permute-start.25 = (f32[192,128]{1,0:T(8,128)S(1)}, f32[192,128]{1,0:T(8,128)S(1)}, u32[]{:S(2)}, u32[]{:S(2)}) collective-permute-start(f32[192,128]{1,0:T(8,128)S(1)} %add_add_fusion.3), channel_id=1, source_target_pairs={{0,48},{1,49},{2,50},{3,51},{8,56},{9,57},{10,58},{11,59}} | collective-permute-start | bytes 294920 | tf_op jit(solution)/shard_map/diag/ppermute | solution.py:35
  29.3 1.3 %collective-permute-start.24 = (f32[192,128]{1,0:T(8,128)S(1)}, f32[192,128]{1,0:T(8,128)S(1)}, u32[]{:S(2)}, u32[]{:S(2)}) collective-permute-start(f32[192,128]{1,0:T(8,128)S(1)} %add_add_fusion.3), channel_id=1, source_target_pairs={{0,16},{1,17},{2,18},{3,19},{8,24},{9,25},{10,26},{11,27}} | collective-permute-start | bytes 294920 | tf_op jit(solution)/shard_map/diag/ppermute | solution.py:35
  30.6 0.0 collective-permute-done.26
  30.6 0.6 collective-permute-start.10
  31.2 0.6 collective-permute-done.25
  31.7 3.7 %collective-permute-start.9 = (f32[128,128]{1,0:T(8,128)S(1)}, f32[128,128]{1,0:T(8,128)S(1)}, u32[]{:S(2)}, u32[]{:S(2)}) collective-permute-start(f32[128,128]{1,0:T(8,128)S(1)} %add_add_fusion.4), channel_id=1, source_target_pairs={{0,128},{1,129},{2,130},{3,131},{4,132},{5,133},{6,134},{7,135},{8... | collective-permute-start | bytes 196616 | tf_op jit(solution)/shard_map/cols/ppermute | solution.py:35
  35.4 2.4 %collective-permute-start.8 = (f32[128,128]{1,0:T(8,128)S(1)}, f32[128,128]{1,0:T(8,128)S(1)}, u32[]{:S(2)}, u32[]{:S(2)}) collective-permute-start(f32[128,128]{1,0:T(8,128)S(1)} %add_add_fusion.4), channel_id=1, source_target_pairs={{0,192},{1,193},{2,194},{3,195},{4,196},{5,197},{6,198},{7,199},{8... | collective-permute-start | bytes 196616 | tf_op jit(solution)/shard_map/cols/ppermute | solution.py:35
  37.8 3.8 %collective-permute-start.29 = (f32[192,128]{1,0:T(8,128)S(1)}, f32[192,128]{1,0:T(8,128)S(1)}, u32[]{:S(2)}, u32[]{:S(2)}) collective-permute-start(f32[192,128]{1,0:T(8,128)S(1)} %add_add_fusion.2), channel_id=1, source_target_pairs={{0,128},{1,129},{2,130},{3,131},{8,136},{9,137},{10,138},{11,139},... | collective-permute-start | bytes 294920 | tf_op jit(solution)/shard_map/diag/ppermute | solution.py:35
  41.6 3.4 %collective-permute-start.28 = (f32[192,128]{1,0:T(8,128)S(1)}, f32[192,128]{1,0:T(8,128)S(1)}, u32[]{:S(2)}, u32[]{:S(2)}) collective-permute-start(f32[192,128]{1,0:T(8,128)S(1)} %add_add_fusion.2), channel_id=1, source_target_pairs={{0,192},{1,193},{2,194},{3,195},{8,200},{9,201},{10,202},{11,203},... | collective-permute-start | bytes 294920 | tf_op jit(solution)/shard_map/diag/ppermute | solution.py:35
  45.0 1.3 %collective-permute-start.27 = (f32[192,128]{1,0:T(8,128)S(1)}, f32[192,128]{1,0:T(8,128)S(1)}, u32[]{:S(2)}, u32[]{:S(2)}) collective-permute-start(f32[192,128]{1,0:T(8,128)S(1)} %add_add_fusion.2), channel_id=1, source_target_pairs={{0,64},{1,65},{2,66},{3,67},{8,72},{9,73},{10,74},{11,75},{16,80},... | collective-permute-start | bytes 294920 | tf_op jit(solution)/shard_map/diag/ppermute | solution.py:35
  46.4 0.1 collective-permute-start.11
  46.5 1.4 %collective-permute-start.12 = (f32[4,128,128]{2,1,0:T(8,128)S(1)}, f32[4,128,128]{2,1,0:T(8,128)S(1)}, u32[]{:S(2)}, u32[]{:S(2)}) collective-permute-start(f32[4,128,128]{2,1,0:T(8,128)S(1)} %pad_maximum_fusion), channel_id=1, source_target_pairs={{0,16},{1,17},{2,18},{3,19},{4,20},{5,21},{6,22},{7,23},{8,24},{9,... | collective-permute-start | bytes 786440 | tf_op jit(solution)/shard_map/cols/ppermute | solution.py:35
  47.9 0.7 collective-permute-start.2
  48.6 1.3 %collective-permute-start.30 = (f32[192,128]{1,0:T(8,128)S(1)}, f32[192,128]{1,0:T(8,128)S(1)}, u32[]{:S(2)}, u32[]{:S(2)}) collective-permute-start(f32[192,128]{1,0:T(8,128)S(1)} %add_add_fusion.1), channel_id=1, source_target_pairs={{0,4},{1,5},{2,6},{3,7},{8,12},{9,13},{10,14},{11,15},{16,20},{17,... | collective-permute-start | bytes 294920 | tf_op jit(solution)/shard_map/diag/ppermute | solution.py:35
  49.9 0.1 pad_add_fusion.pos_ref
  50.0 4.3 %collective-permute-done.12 = f32[4,128,128]{2,1,0:T(8,128)S(1)} collective-permute-done((f32[4,128,128]{2,1,0:T(8,128)S(1)}, f32[4,128,128]{2,1,0:T(8,128)S(1)}, u32[]{:S(2)}, u32[]{:S(2)}) %collective-permute-start.12) | collective-permute-done | bytes 262176 | tf_op jit(solution)/shard_map/cols/ppermute | solution.py:35
  54.3 2.2 %collective-permute-start.15 = (f32[4,128,128]{2,1,0:T(8,128)S(1)}, f32[4,128,128]{2,1,0:T(8,128)S(1)}, u32[]{:S(2)}, u32[]{:S(2)}) collective-permute-start(f32[4,128,128]{2,1,0:T(8,128)S(1)} %pad_maximum_fusion), channel_id=1, source_target_pairs={{0,8},{1,9},{2,10},{3,11},{4,12},{5,13},{6,14},{7,15},{8,0},{9,1},... | collective-permute-start | bytes 786440 | tf_op jit(solution)/shard_map/cols/ppermute | solution.py:35
  56.5 0.2 collective-permute-start.13
  56.7 2.6 %collective-permute-start.14 = (f32[2,128,128]{2,1,0:T(8,128)S(1)}, f32[2,128,128]{2,1,0:T(8,128)S(1)}, u32[]{:S(2)}, u32[]{:S(2)}) collective-permute-start(f32[2,128,128]{2,1,0:T(8,128)S(1)} %slice.62), channel_id=1, source_target_pairs={{0,48},{1,49},{2,50},{3,51},{4,52},{5,53},{6,54},{7,55},{8,56},{9,... | collective-permute-start | bytes 393224 | tf_op jit(solution)/shard_map/cols/ppermute | solution.py:35
  59.4 0.7 collective-permute-start.16
  60.0 0.1 collective-permute-start.18
  60.1 1.0 %add_add_fusion = f32[4,128,128]{2,1,0:T(8,128)S(1)} fusion(f32[4,128,128]{2,1,0:T(8,128)S(1)} %collective-permute-done.2, f32[4,128,128]{2,1,0:T(8,128)S(1)} %collective-permute-done.1, f32[4,128,128]{2,1,0:T(8,128)S(1)} %collective-permute-done, pred[]{:T(512)S(6)} %lt.50, f32[4,128,16,128]{3,1,2,0:T(8,128)} %bitcast.56), kind=kLoop, calls=%fused_computation.2 | loop fusion | flops 262144 | bytes 1310721 | tf_op jit(solution)/shard_map/rows/add | solution.py:229
  61.2 1.7 %collective-permute-done.13 = f32[2,128,128]{2,1,0:T(8,128)S(1)} collective-permute-done((f32[2,128,128]{2,1,0:T(8,128)S(1)}, f32[2,128,128]{2,1,0:T(8,128)S(1)}, u32[]{:S(2)}, u32[]{:S(2)}) %collective-permute-start.13) | collective-permute-done | bytes 131104 | tf_op jit(solution)/shard_map/cols/ppermute | solution.py:35
  62.9 0.8 collective-permute-start.31
  63.7 0.2 collective-permute-start.3
  64.0 0.7 collective-permute-done.31
  64.6 0.4 collective-permute-start.17
  65.1 7.7 %factorize.1 = (f32[256,256]{1,0:T(8,128)S(1)}, f32[256,256]{1,0:T(8,128)S(1)}) custom-call(f32[128,128]{1,0:T(8,128)S(1)} %slice.66.d00_ref, f32[128,128]{1,0:T(8,128)S(1)} %pad_maximum_fusion.1.d01_ref, f32[128,128]{1,0:T(8,128)S(1)} %slice.69.d11_ref), custom_call_target="tpu_custom_call" | custom-call | flops 10000000 | bytes 800000 | tf_op jit(solution)/shard_map/diag/factorize/pallas_call | solution.py:108
  72.9 15.0 %update.1 = f32[8192,128]{1,0:T(8,128)} custom-call(s32[4]{0:T(128)S(1)} %pad_add_fusion.pos_ref, f32[8192,128]{1,0:T(8,128)S(1)} %bitcast.42, f32[512,128]{1,0:T(8,128)S(1)} %bitcast.43, f32[512,128]{1,0:T(8,128)S(1)} %bitcast.51, f32[512,128]{1,0:T(8,128)S(1)} %bitcast.44, f32[512,128]{1,0:T(8,128)S(1)} %bitcast.45, f32[512,128]{1,0:T(8,128)S(1)} %bitcast.47, ...), custom_call_target="tpu_custom_call" | custom-call | flops 5000000000 | bytes 12000000 | tf_op jit(solution)/shard_map/final/update/pallas_call | solution.py:167
  (47 shorter events, 0.4 us)
Async XLA Ops:
  3.5 2.0 %copy-start.1 = (f32[4,1,128,16,1,128]{5,2,3,0,4,1:T(8,128)}, f32[4,1,128,16,1,128]{5,2,3,0,4,1:T(8,128)S(1)}, u32[]{:S(2)}) copy-start(f32[4,1,128,16,1,128]{5,2,3,0,4,1:T(8,128)S(1)} %copy.5) | copy-start | bytes 12582916
  3.5 6.6 %collective-permute-start.19 = (f32[128,128]{1,0:T(8,128)S(1)}, f32[128,128]{1,0:T(8,128)S(1)}, u32[]{:S(2)}, u32[]{:S(2)}) collective-permute-start(f32[128,128]{1,0:T(8,128)S(1)} %slice_bitcast_fusion), channel_id=1, source_target_pairs={{0,1}} | collective-permute-start | bytes 196616 | tf_op jit(solution)/shard_map/diag/ppermute | solution.py:35
  4.2 5.9 %collective-permute-start.20 = (f32[64,128]{1,0:T(8,128)S(1)}, f32[64,128]{1,0:T(8,128)S(1)}, u32[]{:S(2)}, u32[]{:S(2)}) collective-permute-start(f32[64,128]{1,0:T(8,128)S(1)} %get-tuple-element.9), channel_id=1, source_target_pairs={{1,9}} | collective-permute-start | bytes 98312 | tf_op jit(solution)/shard_map/diag/ppermute | solution.py:35
  5.5 40.8 %collective-permute-start.1 = (f32[4,128,128]{2,1,0:T(8,128)S(1)}, f32[4,128,128]{2,1,0:T(8,128)S(1)}, u32[]{:S(2)}, u32[]{:S(2)}) collective-permute-start(f32[4,128,128]{2,1,0:T(8,128)S(1)} %get-tuple-element.12), channel_id=1, source_target_pairs={{0,4},{1,5},{8,12},{9,13},{16,20},{17,21},{24,28},{25,29},{32,36},... | collective-permute-start | bytes 786440 | tf_op jit(solution)/shard_map/rows/ppermute | solution.py:35
  10.1 8.5 %collective-permute-start.23 = (f32[192,128]{1,0:T(8,128)S(1)}, f32[192,128]{1,0:T(8,128)S(1)}, u32[]{:S(2)}, u32[]{:S(2)}) collective-permute-start(f32[192,128]{1,0:T(8,128)S(1)} %fusion), channel_id=1, source_target_pairs={{1,3},{9,11}} | collective-permute-start | bytes 294920 | tf_op jit(solution)/shard_map/diag/ppermute | solution.py:35
  10.8 9.7 %collective-permute-start.22 = (f32[192,128]{1,0:T(8,128)S(1)}, f32[192,128]{1,0:T(8,128)S(1)}, u32[]{:S(2)}, u32[]{:S(2)}) collective-permute-start(f32[192,128]{1,0:T(8,128)S(1)} %fusion), channel_id=1, source_target_pairs={{1,0},{9,8}} | collective-permute-start | bytes 294920 | tf_op jit(solution)/shard_map/diag/ppermute | solution.py:35
  12.1 11.3 %collective-permute-start.21 = (f32[192,128]{1,0:T(8,128)S(1)}, f32[192,128]{1,0:T(8,128)S(1)}, u32[]{:S(2)}, u32[]{:S(2)}) collective-permute-start(f32[192,128]{1,0:T(8,128)S(1)} %fusion), channel_id=1, source_target_pairs={{1,2},{9,10}} | collective-permute-start | bytes 294920 | tf_op jit(solution)/shard_map/diag/ppermute | solution.py:35
  12.8 11.9 %collective-permute-start.7 = (f32[128,128]{1,0:T(8,128)S(1)}, f32[128,128]{1,0:T(8,128)S(1)}, u32[]{:S(2)}, u32[]{:S(2)}) collective-permute-start(f32[128,128]{1,0:T(8,128)S(1)} %get-tuple-element.20), channel_id=1, source_target_pairs={{0,48},{1,56},{8,49},{9,57},{16,2},{17,10},{24,3},{25,11},{32,20},... | collective-permute-start | bytes 196616 | tf_op jit(solution)/shard_map/cols/ppermute | solution.py:35
  18.6 54.3 %copy-start = (f32[4,1,128,16,1,128]{5,4,3,2,1,0:T(1,128)S(1)}, f32[4,1,128,16,1,128]{5,4,3,2,1,0:T(1,128)}, u32[]{:S(2)}) copy-start(f32[4,1,128,16,1,128]{5,4,3,2,1,0:T(1,128)} %param.1) | copy-start | bytes 12582916
  18.6 7.4 %collective-permute-start.6 = (f32[128,128]{1,0:T(8,128)S(1)}, f32[128,128]{1,0:T(8,128)S(1)}, u32[]{:S(2)}, u32[]{:S(2)}) collective-permute-start(f32[128,128]{1,0:T(8,128)S(1)} %get-tuple-element.18), channel_id=1, source_target_pairs={{0,32},{1,40},{8,33},{9,41},{16,50},{17,58},{24,51},{25,59},{32,4}... | collective-permute-start | bytes 196616 | tf_op jit(solution)/shard_map/cols/ppermute | solution.py:35
  20.5 7.4 %collective-permute-start.4 = (f32[128,128]{1,0:T(8,128)S(1)}, f32[128,128]{1,0:T(8,128)S(1)}, u32[]{:S(2)}, u32[]{:S(2)}) collective-permute-start(f32[128,128]{1,0:T(8,128)S(1)} %get-tuple-element.19), channel_id=1, source_target_pairs={{0,0},{1,8},{8,1},{9,9},{16,18},{17,26},{24,19},{25,27},{32,36},{3... | collective-permute-start | bytes 196616 | tf_op jit(solution)/shard_map/cols/ppermute | solution.py:35
  23.4 5.9 %collective-permute-start.5 = (f32[128,128]{1,0:T(8,128)S(1)}, f32[128,128]{1,0:T(8,128)S(1)}, u32[]{:S(2)}, u32[]{:S(2)}) collective-permute-start(f32[128,128]{1,0:T(8,128)S(1)} %get-tuple-element.17), channel_id=1, source_target_pairs={{0,16},{1,24},{8,17},{9,25},{16,34},{17,42},{24,35},{25,43},{32,52... | collective-permute-start | bytes 196616 | tf_op jit(solution)/shard_map/cols/ppermute | solution.py:35
  24.7 34.7 %collective-permute-start = (f32[4,128,128]{2,1,0:T(8,128)S(1)}, f32[4,128,128]{2,1,0:T(8,128)S(1)}, u32[]{:S(2)}, u32[]{:S(2)}) collective-permute-start(f32[4,128,128]{2,1,0:T(8,128)S(1)} %get-tuple-element.12), channel_id=1, source_target_pairs={{0,3},{1,2},{8,11},{9,10},{16,19},{17,18},{24,27},{25,26},{32,35},... | collective-permute-start | bytes 786440 | tf_op jit(solution)/shard_map/rows/ppermute | solution.py:35
  26.0 4.6 %collective-permute-start.26 = (f32[192,128]{1,0:T(8,128)S(1)}, f32[192,128]{1,0:T(8,128)S(1)}, u32[]{:S(2)}, u32[]{:S(2)}) collective-permute-start(f32[192,128]{1,0:T(8,128)S(1)} %add_add_fusion.3), channel_id=1, source_target_pairs={{0,32},{1,33},{2,34},{3,35},{8,40},{9,41},{10,42},{11,43}} | collective-permute-start | bytes 294920 | tf_op jit(solution)/shard_map/diag/ppermute | solution.py:35
  27.9 3.8 %collective-permute-start.25 = (f32[192,128]{1,0:T(8,128)S(1)}, f32[192,128]{1,0:T(8,128)S(1)}, u32[]{:S(2)}, u32[]{:S(2)}) collective-permute-start(f32[192,128]{1,0:T(8,128)S(1)} %add_add_fusion.3), channel_id=1, source_target_pairs={{0,48},{1,49},{2,50},{3,51},{8,56},{9,57},{10,58},{11,59}} | collective-permute-start | bytes 294920 | tf_op jit(solution)/shard_map/diag/ppermute | solution.py:35
  29.3 6.1 %collective-permute-start.24 = (f32[192,128]{1,0:T(8,128)S(1)}, f32[192,128]{1,0:T(8,128)S(1)}, u32[]{:S(2)}, u32[]{:S(2)}) collective-permute-start(f32[192,128]{1,0:T(8,128)S(1)} %add_add_fusion.3), channel_id=1, source_target_pairs={{0,16},{1,17},{2,18},{3,19},{8,24},{9,25},{10,26},{11,27}} | collective-permute-start | bytes 294920 | tf_op jit(solution)/shard_map/diag/ppermute | solution.py:35
  30.6 7.2 %collective-permute-start.10 = (f32[128,128]{1,0:T(8,128)S(1)}, f32[128,128]{1,0:T(8,128)S(1)}, u32[]{:S(2)}, u32[]{:S(2)}) collective-permute-start(f32[128,128]{1,0:T(8,128)S(1)} %add_add_fusion.4), channel_id=1, source_target_pairs={{0,64},{1,65},{2,66},{3,67},{4,68},{5,69},{6,70},{7,71},{8,72},{9,... | collective-permute-start | bytes 196616 | tf_op jit(solution)/shard_map/cols/ppermute | solution.py:35
  31.7 9.9 %collective-permute-start.9 = (f32[128,128]{1,0:T(8,128)S(1)}, f32[128,128]{1,0:T(8,128)S(1)}, u32[]{:S(2)}, u32[]{:S(2)}) collective-permute-start(f32[128,128]{1,0:T(8,128)S(1)} %add_add_fusion.4), channel_id=1, source_target_pairs={{0,128},{1,129},{2,130},{3,131},{4,132},{5,133},{6,134},{7,135},{8... | collective-permute-start | bytes 196616 | tf_op jit(solution)/shard_map/cols/ppermute | solution.py:35
  35.4 9.6 %collective-permute-start.8 = (f32[128,128]{1,0:T(8,128)S(1)}, f32[128,128]{1,0:T(8,128)S(1)}, u32[]{:S(2)}, u32[]{:S(2)}) collective-permute-start(f32[128,128]{1,0:T(8,128)S(1)} %add_add_fusion.4), channel_id=1, source_target_pairs={{0,192},{1,193},{2,194},{3,195},{4,196},{5,197},{6,198},{7,199},{8... | collective-permute-start | bytes 196616 | tf_op jit(solution)/shard_map/cols/ppermute | solution.py:35
  37.8 8.6 %collective-permute-start.29 = (f32[192,128]{1,0:T(8,128)S(1)}, f32[192,128]{1,0:T(8,128)S(1)}, u32[]{:S(2)}, u32[]{:S(2)}) collective-permute-start(f32[192,128]{1,0:T(8,128)S(1)} %add_add_fusion.2), channel_id=1, source_target_pairs={{0,128},{1,129},{2,130},{3,131},{8,136},{9,137},{10,138},{11,139},... | collective-permute-start | bytes 294920 | tf_op jit(solution)/shard_map/diag/ppermute | solution.py:35
  41.6 6.3 %collective-permute-start.28 = (f32[192,128]{1,0:T(8,128)S(1)}, f32[192,128]{1,0:T(8,128)S(1)}, u32[]{:S(2)}, u32[]{:S(2)}) collective-permute-start(f32[192,128]{1,0:T(8,128)S(1)} %add_add_fusion.2), channel_id=1, source_target_pairs={{0,192},{1,193},{2,194},{3,195},{8,200},{9,201},{10,202},{11,203},... | collective-permute-start | bytes 294920 | tf_op jit(solution)/shard_map/diag/ppermute | solution.py:35
  45.0 3.6 %collective-permute-start.27 = (f32[192,128]{1,0:T(8,128)S(1)}, f32[192,128]{1,0:T(8,128)S(1)}, u32[]{:S(2)}, u32[]{:S(2)}) collective-permute-start(f32[192,128]{1,0:T(8,128)S(1)} %add_add_fusion.2), channel_id=1, source_target_pairs={{0,64},{1,65},{2,66},{3,67},{8,72},{9,73},{10,74},{11,75},{16,80},... | collective-permute-start | bytes 294920 | tf_op jit(solution)/shard_map/diag/ppermute | solution.py:35
  46.4 10.1 %collective-permute-start.11 = (f32[4,128,128]{2,1,0:T(8,128)S(1)}, f32[4,128,128]{2,1,0:T(8,128)S(1)}, u32[]{:S(2)}, u32[]{:S(2)}) collective-permute-start(f32[4,128,128]{2,1,0:T(8,128)S(1)} %pad_maximum_fusion), channel_id=1, source_target_pairs={{0,48},{1,49},{2,50},{3,51},{4,52},{5,53},{6,54},{7,55},{8,56},{9,... | collective-permute-start | bytes 786440 | tf_op jit(solution)/shard_map/cols/ppermute | solution.py:35
  46.5 7.8 %collective-permute-start.12 = (f32[4,128,128]{2,1,0:T(8,128)S(1)}, f32[4,128,128]{2,1,0:T(8,128)S(1)}, u32[]{:S(2)}, u32[]{:S(2)}) collective-permute-start(f32[4,128,128]{2,1,0:T(8,128)S(1)} %pad_maximum_fusion), channel_id=1, source_target_pairs={{0,16},{1,17},{2,18},{3,19},{4,20},{5,21},{6,22},{7,23},{8,24},{9,... | collective-permute-start | bytes 786440 | tf_op jit(solution)/shard_map/cols/ppermute | solution.py:35
  47.9 12.1 %collective-permute-start.2 = (f32[4,128,128]{2,1,0:T(8,128)S(1)}, f32[4,128,128]{2,1,0:T(8,128)S(1)}, u32[]{:S(2)}, u32[]{:S(2)}) collective-permute-start(f32[4,128,128]{2,1,0:T(8,128)S(1)} %collective-permute-done.1), channel_id=1, source_target_pairs={{4,7},{5,6},{12,15},{13,14},{20,23},{21,22},{28,31},{29,30},{36,39... | collective-permute-start | bytes 786440 | tf_op jit(solution)/shard_map/rows/ppermute | solution.py:35
  48.6 8.1 %collective-permute-start.30 = (f32[192,128]{1,0:T(8,128)S(1)}, f32[192,128]{1,0:T(8,128)S(1)}, u32[]{:S(2)}, u32[]{:S(2)}) collective-permute-start(f32[192,128]{1,0:T(8,128)S(1)} %add_add_fusion.1), channel_id=1, source_target_pairs={{0,4},{1,5},{2,6},{3,7},{8,12},{9,13},{10,14},{11,15},{16,20},{17,... | collective-permute-start | bytes 294920 | tf_op jit(solution)/shard_map/diag/ppermute | solution.py:35
  54.3 18.6 %collective-permute-start.15 = (f32[4,128,128]{2,1,0:T(8,128)S(1)}, f32[4,128,128]{2,1,0:T(8,128)S(1)}, u32[]{:S(2)}, u32[]{:S(2)}) collective-permute-start(f32[4,128,128]{2,1,0:T(8,128)S(1)} %pad_maximum_fusion), channel_id=1, source_target_pairs={{0,8},{1,9},{2,10},{3,11},{4,12},{5,13},{6,14},{7,15},{8,0},{9,1},... | collective-permute-start | bytes 786440 | tf_op jit(solution)/shard_map/cols/ppermute | solution.py:35
  56.5 6.4 %collective-permute-start.13 = (f32[2,128,128]{2,1,0:T(8,128)S(1)}, f32[2,128,128]{2,1,0:T(8,128)S(1)}, u32[]{:S(2)}, u32[]{:S(2)}) collective-permute-start(f32[2,128,128]{2,1,0:T(8,128)S(1)} %slice.61), channel_id=1, source_target_pairs={{0,16},{1,17},{2,18},{3,19},{4,20},{5,21},{6,22},{7,23},{8,24},{9,... | collective-permute-start | bytes 393224 | tf_op jit(solution)/shard_map/cols/ppermute | solution.py:35
  56.7 7.0 %collective-permute-start.14 = (f32[2,128,128]{2,1,0:T(8,128)S(1)}, f32[2,128,128]{2,1,0:T(8,128)S(1)}, u32[]{:S(2)}, u32[]{:S(2)}) collective-permute-start(f32[2,128,128]{2,1,0:T(8,128)S(1)} %slice.62), channel_id=1, source_target_pairs={{0,48},{1,49},{2,50},{3,51},{4,52},{5,53},{6,54},{7,55},{8,56},{9,... | collective-permute-start | bytes 393224 | tf_op jit(solution)/shard_map/cols/ppermute | solution.py:35
  59.4 13.5 %collective-permute-start.16 = (f32[4,128,128]{2,1,0:T(8,128)S(1)}, f32[4,128,128]{2,1,0:T(8,128)S(1)}, u32[]{:S(2)}, u32[]{:S(2)}) collective-permute-start(f32[4,128,128]{2,1,0:T(8,128)S(1)} %collective-permute-done.11), channel_id=1, source_target_pairs={{0,8},{1,9},{2,10},{3,11},{4,12},{5,13},{6,14},{7,15},{8,0},{9,1},... | collective-permute-start | bytes 786440 | tf_op jit(solution)/shard_map/cols/ppermute | solution.py:35
  60.0 12.8 %collective-permute-start.18 = (f32[4,128,128]{2,1,0:T(8,128)S(1)}, f32[4,128,128]{2,1,0:T(8,128)S(1)}, u32[]{:S(2)}, u32[]{:S(2)}) collective-permute-start(f32[4,128,128]{2,1,0:T(8,128)S(1)} %collective-permute-done.12), channel_id=1, source_target_pairs={{0,8},{1,9},{2,10},{3,11},{4,12},{5,13},{6,14},{7,15},{8,0},{9,1},... | collective-permute-start | bytes 786440 | tf_op jit(solution)/shard_map/cols/ppermute | solution.py:35
  62.9 1.7 %collective-permute-start.31 = (f32[192,128]{1,0:T(8,128)S(1)}, f32[192,128]{1,0:T(8,128)S(1)}, u32[]{:S(2)}, u32[]{:S(2)}) collective-permute-start(f32[192,128]{1,0:T(8,128)S(1)} %add.123), channel_id=1, source_target_pairs={{0,8},{1,9},{2,10},{3,11},{4,12},{5,13},{6,14},{7,15},{8,0},{9,1},... | collective-permute-start | bytes 294920 | tf_op jit(solution)/shard_map/diag/ppermute | solution.py:35
  63.7 9.2 %collective-permute-start.3 = (f32[4,128,128]{2,1,0:T(8,128)S(1)}, f32[4,128,128]{2,1,0:T(8,128)S(1)}, u32[]{:S(2)}, u32[]{:S(2)}) collective-permute-start(f32[4,128,128]{2,1,0:T(8,128)S(1)} %add_add_fusion), channel_id=1, source_target_pairs={{0,1},{1,0},{2,3},{3,2},{4,5},{5,4},{6,7},{7,6},{8,9},{9,8},{10,11... | collective-permute-start | bytes 786440 | tf_op jit(solution)/shard_map/rows/ppermute | solution.py:35
  64.6 8.3 %collective-permute-start.17 = (f32[4,128,128]{2,1,0:T(8,128)S(1)}, f32[4,128,128]{2,1,0:T(8,128)S(1)}, u32[]{:S(2)}, u32[]{:S(2)}) collective-permute-start(f32[4,128,128]{2,1,0:T(8,128)S(1)} %constant_dynamic-update-slice_fusion), channel_id=1, source_target_pairs={{0,8},{1,9},{2,10},{3,11},{4,12},{5,13},{6,14},{7,15},{8,0},{9,1},... | collective-permute-start | bytes 786440 | tf_op jit(solution)/shard_map/cols/ppermute | solution.py:35

commit v2 on v1

v2 whole, which is shorter than its diff:
```python
import functools

import jax
import jax.numpy as jnp
from jax import lax
from jax.experimental import pallas as pl
from jax.experimental.pallas import tpu as pltpu
from jax.sharding import PartitionSpec as P

HIGHEST = lax.Precision.HIGHEST
BLK = 128
PANEL = 2 * BLK
AXES = ("row", "col")


def device_id(zh, y, core, zl, x):
    return ((zh % 4) * 8 + (y % 4) * 2 + core) * 8 + zl * 4 + x % 4


def all_places():
    for zh in range(4):
        for y in range(4):
            for core in range(2):
                for zl in range(2):
                    for x in range(4):
                        yield zh, y, core, zl, x


def pairs_of(target):
    pairs = {}
    for place in all_places():
        to = target(*place)
        if to is not None:
            pairs[device_id(*place)] = device_id(*to)
    return pairs


def closed(pairs):
    source = {to: at for at, to in pairs.items()}
    out = dict(pairs)
    for end in source:
        if end not in pairs:
            start = end
            while start in source:
                start = source[start]
            out[end] = start
    used = set(out) | set(out.values())
    for at in range(256):
        sibling = at ^ 8
        if at not in used and sibling not in used:
            out[at] = sibling
    return sorted(out.items())


def send(value, target):
    return lax.ppermute(value, AXES, closed(pairs_of(target)))


def spread(which, value, payloads, targets):
    got = [send(p, t) for p, t in zip(payloads, targets)]
    for i, v in enumerate(got):
        value = v if value is None else jnp.where(which == i + 1, v, value)
    return value


def dot(a, b, contract):
    return lax.dot_general(a, b, (contract, ((), ())), preferred_element_type=jnp.float32)


def dot_tn(a, b):
    return lax.dot_general(
        a, b, (((0,), (0,)), ((), ())), precision=HIGHEST, preferred_element_type=jnp.float32
    )


def halves(v):
    high = v.astype(jnp.bfloat16)
    return high, (v - high.astype(jnp.float32)).astype(jnp.bfloat16)


def dot_pairs(pairs):
    left, right = [], []
    for a, b in pairs:
        ah, al = halves(a)
        bh, bl = halves(b)
        left += [ah, ah, al]
        right += [bh, bl, bh]
    return dot(jnp.concatenate(left, 1), jnp.concatenate(right, 1), ((1,), (1,)))


def prepare_kernel(pos_ref, a_ref, left_ref, p0_ref, p1_ref, p2_ref, p3_ref):
    left_ref[...] = a_ref[:, 0, :]
    y = pos_ref[2]
    for s, p_ref in enumerate((p0_ref, p1_ref, p2_ref, p3_ref)):
        block = lax.rem(y + s, 4)
        p_ref[...] = left_ref[pl.ds(pl.multiple_of(block * BLK, BLK), BLK), :]


def prepare(pos, a):
    vmem = pl.BlockSpec(memory_space=pltpu.VMEM)
    block = jax.ShapeDtypeStruct((BLK, BLK), jnp.float32)
    return pl.pallas_call(
        prepare_kernel,
        grid=(1,),
        out_shape=[jax.ShapeDtypeStruct((512, BLK), jnp.float32)] + [block] * 4,
        in_specs=[
            pl.BlockSpec(memory_space=pltpu.SMEM),
            pl.BlockSpec((512, 8, BLK), lambda i: (0, 0, 0)),
        ],
        out_specs=[vmem] * 5,
        compiler_params=pltpu.CompilerParams(vmem_limit_bytes=24 * 1024 * 1024),
        name="prepare",
    )(pos, a.reshape(512, 16, BLK))

def factor_kernel(nb, pos_ref, own_ref, across_ref, core_ref, both_ref, u_ref, w_ref, m_ref, d00_ref, d01_ref, d11_ref):
    even, low = pos_ref[4] == 0, pos_ref[5] == 1
    left_mine = jnp.where(low, own_ref[...], across_ref[...])
    right_mine = jnp.where(low, across_ref[...], own_ref[...])
    left_other = jnp.where(low, core_ref[...], both_ref[...])
    right_other = jnp.where(low, both_ref[...], core_ref[...])
    d00_ref[...] = jnp.where(even, left_mine, left_other)
    d01_ref[...] = jnp.where(even, right_mine, right_other)
    d11_ref[...] = jnp.where(even, right_other, right_mine)
    lane = lax.broadcasted_iota(jnp.int32, (nb, BLK), 1)
    sub = lax.broadcasted_iota(jnp.int32, (nb, BLK), 0)
    for p in range(PANEL // nb):
        k0 = p * nb
        half = k0 // BLK
        c0 = k0 % BLK
        if half == 0:
            tiles = [d00_ref[k0 : k0 + nb, :], d01_ref[k0 : k0 + nb, :]]
        else:
            tiles = [None, d11_ref[c0 : c0 + nb, :]]
        for t in range(2):
            one = jnp.where(lane + t * BLK == sub + k0, 1.0, 0.0)
            tiles.append(one if t <= half else None)
        if p > 0:
            lhs = m_ref[0:k0, k0 : k0 + nb]
            for t in range(4):
                if tiles[t] is not None:
                    tiles[t] = tiles[t] - dot_tn(lhs, m_ref[0:k0, t * BLK : (t + 1) * BLK])
        spread = [
            jnp.broadcast_to(tiles[half][:, c0 + j : c0 + j + 1], (nb, BLK)) for j in range(nb)
        ]
        pivots = jnp.ones((nb, BLK), jnp.float32)
        for k in range(nb):
            column = spread[k]
            pivot = jnp.broadcast_to(column[k : k + 1, :], (nb, BLK))
            pivots = jnp.where(sub == k, pivot, pivots)
            if k < nb - 1:
                ratio = jnp.where(sub > k, column, 0.0) * (1.0 / pivot)
                for j in range(k + 1, nb):
                    spread[j] = spread[j] - ratio * jnp.broadcast_to(column[j : j + 1, :], (nb, BLK))
                for t in range(4):
                    if tiles[t] is not None:
                        tiles[t] = tiles[t] - ratio * jnp.broadcast_to(
                            tiles[t][k : k + 1, :], (nb, BLK)
                        )
        scale = lax.rsqrt(pivots)
        for t in range(4):
            if tiles[t] is None:
                out = jnp.zeros((nb, BLK), jnp.float32)
            else:
                out = tiles[t] * scale
                if t == half:
                    out = jnp.where(lane >= sub + c0, out, 0.0)
            m_ref[k0 : k0 + nb, t * BLK : (t + 1) * BLK] = out
    u_ref[...] = m_ref[:, :PANEL]
    w_ref[...] = m_ref[:, PANEL:]


def factorize(pos, own, across, core, both):
    square = jax.ShapeDtypeStruct((PANEL, PANEL), jnp.float32)
    vmem = pl.BlockSpec(memory_space=pltpu.VMEM)
    return pl.pallas_call(
        functools.partial(factor_kernel, 32),
        out_shape=[square, square],
        in_specs=[pl.BlockSpec(memory_space=pltpu.SMEM)] + [vmem] * 4,
        out_specs=[vmem] * 2,
        scratch_shapes=[pltpu.VMEM((PANEL, 2 * PANEL), jnp.float32)]
        + [pltpu.VMEM((BLK, BLK), jnp.float32)] * 3,
        compiler_params=pltpu.CompilerParams(vmem_limit_bytes=24 * 1024 * 1024),
        cost_estimate=pl.CostEstimate(flops=4000000000, bytes_accessed=800000, transcendentals=0),
        name="factorize",
    )(pos, own, across, core, both)


def update_kernel(rows, pos_ref, a_ref, near_ref, far_ref, *refs):
    mine = refs[0:4]
    other = refs[4:8]
    w_ref, u_ref, o_ref = refs[8:11]
    thigh_ref, tlow_ref, shigh_ref, slow_ref, top_ref, left_ref, sum_ref = refs[11:]
    step = pl.program_id(0)
    row, col, y, zh = pos_ref[0], pos_ref[1], pos_ref[2], pos_ref[3]
    even, low = pos_ref[4] == 0, pos_ref[5] == 1

    @pl.when(step == 0)
    def _():
        wlo, whi = w_ref[:, :BLK], w_ref[:, BLK:]
        wnear, wfar = jnp.where(low, wlo, whi), jnp.where(low, whi, wlo)
        solved = dot_pairs([(near_ref[...], wnear), (far_ref[...], wfar)])
        shigh_ref[...], slow_ref[...] = halves(solved)
        left_ref[...] = jnp.where(col == 0, solved[:, :BLK], solved[:, BLK:])
        wmine, wother = jnp.where(even, wlo, whi), jnp.where(even, whi, wlo)
        for d in range(4):
            solved = dot_pairs([(wmine, mine[d][...]), (wother, other[d][...])])
            high, lower = halves(solved)
            for k in range(4):
                j = 4 * lax.rem(y + d, 4) + lax.rem(zh + k, 4)
                at = pl.ds(pl.multiple_of(j * BLK, BLK), BLK)
                thigh_ref[:, at] = high[:, k * BLK : (k + 1) * BLK]
                tlow_ref[:, at] = lower[:, k * BLK : (k + 1) * BLK]

                @pl.when(row < 2)
                def _():
                    block = solved[:, k * BLK : (k + 1) * BLK]
                    top_ref[:, at] = jnp.where(row == 0, block[:BLK], block[BLK:])

    at = pl.ds(pl.multiple_of(step * rows, rows), rows)
    shigh, slow = shigh_ref[at, :], slow_ref[at, :]
    wide = jnp.concatenate([shigh, shigh, slow], 1)
    for n in range(8):
        cut = slice(n * 256, (n + 1) * 256)
        thigh, tlow = thigh_ref[:, cut], tlow_ref[:, cut]
        sum_ref[:, cut] = dot(wide, jnp.concatenate([thigh, tlow, thigh], 0), ((1,), (0,)))
    o_ref[...] = a_ref[...] - sum_ref[...].reshape(rows, 16, BLK).reshape(rows * 16, BLK)

    @pl.when((row < 2) & (step == 0))
    def _():
        o_ref[: BLK * 16, :] = top_ref[...].reshape(BLK, 16, BLK).reshape(BLK * 16, BLK)

    @pl.when(col < 2)
    def _():
        o_ref[pl.ds(0, rows, 16), :] = left_ref[at, :]

    @pl.when((row < 2) & (col < 2) & (step == 0))
    def _():
        strip = u_ref[pl.ds(pl.multiple_of(col * BLK, BLK), BLK), :]
        o_ref[pl.ds(0, BLK, 16), :] = jnp.where(row == 0, strip[:, :BLK], strip[:, BLK:]).T


def update(pos, a, near, far, mine, other, inverse, upper):
    rows = 2 * BLK
    vmem = pl.BlockSpec(memory_space=pltpu.VMEM)
    tile = pl.BlockSpec((rows * 16, BLK), lambda i: (i, 0))
    return pl.pallas_call(
        functools.partial(update_kernel, rows),
        grid=(512 // rows,),
        out_shape=jax.ShapeDtypeStruct(a.shape, jnp.float32),
        in_specs=[pl.BlockSpec(memory_space=pltpu.SMEM), tile] + [vmem] * 12,
        out_specs=tile,
        scratch_shapes=[
            pltpu.VMEM((PANEL, 2048), jnp.bfloat16),
            pltpu.VMEM((PANEL, 2048), jnp.bfloat16),
            pltpu.VMEM((512, PANEL), jnp.bfloat16),
            pltpu.VMEM((512, PANEL), jnp.bfloat16),
            pltpu.VMEM((BLK, 2048), jnp.float32),
            pltpu.VMEM((512, BLK), jnp.float32),
            pltpu.VMEM((rows, 2048), jnp.float32),
        ],
        compiler_params=pltpu.CompilerParams(vmem_limit_bytes=40 * 1024 * 1024),
        cost_estimate=pl.CostEstimate(
            flops=3000000000, bytes_accessed=12000000, transcendentals=0
        ),
        name="update",
    )(pos, a, near, far, *mine, *other, inverse, upper)


def local(kernel):
    row = lax.axis_index("row")
    col = lax.axis_index("col")
    zh, y, core = row // 8, (row // 2) % 4, row % 2
    zl, x = col // 4, col % 4
    low = (x == 0) | (x == 3)
    pos = jnp.stack([row, col, y, zh, core, low.astype(row.dtype)]).astype(jnp.int32)
    flat = kernel.reshape(512 * 16, BLK)
    left, p0, p1, p2, p3 = prepare(pos, flat)

    with jax.named_scope("rows"):
        held = spread(zl, left, [left], [lambda zh, y, core, zl, x: (zh, y, core, 1, x) if zl == 0 and x < 2 else None])
        near = spread(x >> 1, held, [held], [lambda zh, y, core, zl, x: (zh, y, core, zl, 3 - x) if x < 2 else None])

    with jax.named_scope("diag"):
        diag = left[:BLK]
        root = lambda zh, y, zl, x: (zh, y, zl) == (0, 0, 0) and x < 2
        stages = [
            [
                lambda zh, y, core, zl, x, t=t, m=m: (0, 0, core, t, 3 - x if m else x) if root(zh, y, zl, x) else None
                for t, m in ((0, True), (1, False), (1, True))
            ],
            [
                lambda zh, y, core, zl, x, s=s: (0, y + s, core, zl, x) if (zh, y) == (0, 0) else None
                for s in (1, 3, 2)
            ],
            [
                lambda zh, y, core, zl, x, s=s: (zh + s, y, core, zl, x) if zh == 0 else None
                for s in (1, 3, 2)
            ],
        ]
        near_pair = (x >> 1) + 2 * zl
        arrivals = [
            jnp.where((zh == 0) & (y == 0), near_pair, 0),
            jnp.where(zh == 0, jnp.where(y == 0, 0, jnp.where(y == 1, 1, jnp.where(y == 3, 2, 3))), 0),
            jnp.where(zh == 0, 0, jnp.where(zh == 1, 1, jnp.where(zh == 3, 2, 3))),
        ]
        for which, targets in zip(arrivals, stages):
            diag = spread(which, diag, [diag] * 3, targets)
        diag, near = lax.optimization_barrier((diag, near))
        across = send(diag, lambda zh, y, core, zl, x: (zh, y, core, zl, x ^ 1))
        both = send(diag, lambda zh, y, core, zl, x: (zh, y, 1 - core, zl, x ^ 1))
        cored = send(diag, lambda zh, y, core, zl, x: (zh, y, 1 - core, zl, x))
        far = send(near, lambda zh, y, core, zl, x: (zh, y, core, zl, x ^ 1))
        upper, inverse = factorize(pos, diag, across, cored, both)

    with jax.named_scope("cols"):
        piece = spread(
            lax.rem(y - (col >> 1) + 4, 4) + 1,
            None,
            [p0, p1, p2, p3],
            [
                lambda zh, y, core, zl, x, s=s: (zh, y + s, x, y // 2, 2 * (y % 2) + core)
                if zl == 0 and x < 2
                else None
                for s in range(4)
            ],
        )
        over_z = [piece] + [
            send(piece, lambda zh, y, core, zl, x, s=s: (zh - s, y, core, zl, x)) for s in (1, 2, 3)
        ]
        own = jnp.concatenate(over_z)
        around = [
            send(own, lambda zh, y, core, zl, x, s=s: (zh, y - s, core, zl, x)) for s in (1, 2, 3)
        ]
        *around, inverse = lax.optimization_barrier((*around, inverse))
        mine = [own] + around
        other = [send(v, lambda zh, y, core, zl, x: (zh, y, 1 - core, zl, x)) for v in mine]

    with jax.named_scope("final"):
        out = update(pos, flat, near, far, mine, other, inverse, upper)
    return out.reshape(kernel.shape)


def solution(mesh):
    placed = P(None, "row", None, None, "col", None)
    return jax.shard_map(
        local, mesh=mesh, in_specs=(placed,), out_specs=placed, check_vma=False
    )
```

time: 88.4 us -> 67.3 us (0.76)
  starting transfers between devices: 51.6 us -> 34.5 us
  waiting for transfers between devices: 7.33 us -> 13.9 us
  Pallas kernels: 22.7 us -> 16.3 us
  local copies, waits for them, and re-layouts: 4.25 us -> 2.29 us
  other arithmetic: 1.31 us -> 0.14 us
    ppermute x32 -> x29, starting transfers between devices: 51.6 us -> 34.5 us  [send(): return lax.ppermute(value, AXES, closed(pairs_of(target)))]
    pallas_call x1 -> x2, Pallas kernels: 15 us -> 7.99 us  [the longest x1 7.27 us: update(): pl.pallas_call(functools.partial(update_kernel, rows), grid=(512 // rows,...]
    ppermute x32 -> x29, waiting for transfers between devices: 7.33 us -> 13.9 us  [send(): return lax.ppermute(value, AXES, closed(pairs_of(target)))]
    unnamed x6 -> x4, local copies, waits for them, and re-layouts: 4.12 us -> 2.2 us
    add x6 -> x0, other arithmetic: 1.13 us -> none  [the longest x1 1.03 us: local(): near = jnp.where(col < 2, left, 0.0) + r1 + r2 + r3]
  transfers between devices with their start and end apart: 32 -> 29, of which waited for: 4 -> 9; matrix products, arithmetic and copies ran while one was open for 2% -> 0% of each run, Pallas kernels for 9% -> 12%
where the time goes in v2:
time: 67.3 us; the launch traced here: 67.2 us
  starting transfers between devices  34.5 us (51%)
  Pallas kernels  16.3 us (24%)
  waiting for transfers between devices  13.9 us (21%)
  local copies, waits for them, and re-layouts  2.29 us (3%)
    ppermute x29, starting transfers between devices, send(): return lax.ppermute(value, AXES, closed(pairs_of(target)))  34.5 us
    ppermute x29, waiting for transfers between devices, send(): return lax.ppermute(value, AXES, closed(pairs_of(target)))  13.9 us
    pallas_call x1, Pallas kernels, factorize(): pl.pallas_call(functools.partial(factor_kernel, 32), out_shape=[square, s...  8.27 us
    pallas_call x1, Pallas kernels, update(): pl.pallas_call(functools.partial(update_kernel, rows), grid=(512 // rows,...  7.27 us
    unnamed x4, local copies, waits for them, and re-layouts  2.2 us
  transfers between devices with their start and end apart: 29, of which 9 were waited for; matrix products, arithmetic and copies ran while one was open for 0% of the time, Pallas kernels for 12%

profile of v2, /device:TPU:1, one launch (start us, length us, event | category | flops | bytes accessed | tf_op | source)
XLA Modules:
  0.0 67.2 jit_solution(7215235994404961093)
XLA Ops:
  0.0 0.1 stack.31.pos_ref
  0.1 2.2 %copy-done = f32[4,1,128,16,1,128]{5,4,3,2,1,0:T(1,128)S(1)} copy-done((f32[4,1,128,16,1,128]{5,4,3,2,1,0:T(1,128)S(1)}, f32[4,1,128,16,1,128]{5,4,3,2,1,0:T(1,128)}, u32[]{:S(2)}) %copy-start) | copy-done | bytes 4194328
  2.3 0.7 %prepare.1 = (f32[512,128]{1,0:T(8,128)S(1)}, f32[128,128]{1,0:T(8,128)S(1)}, f32[128,128]{1,0:T(8,128)S(1)}, f32[128,128]{1,0:T(8,128)S(1)}, f32[128,128]{1,0:T(8,128)S(1)}) custom-call(s32[6]{0:T(128)S(1)} %stack.31.pos_ref, f32[512,16,128]{2,1,0:T(8,128)S(1)} %bitcast.11), custom_call_target="tpu_custom_call" | custom-call | tf_op jit(solution)/shard_map/prepare/pallas_call | solution.py:102
  3.0 3.4 %collective-permute-start.2 = (f32[128,128]{1,0:T(8,128)S(1)}, f32[128,128]{1,0:T(8,128)S(1)}, u32[]{:S(2)}, u32[]{:S(2)}) collective-permute-start(f32[128,128]{1,0:T(8,128)S(1)} %slice.3), channel_id=1, source_target_pairs={{0,3},{1,2},{2,1},{3,0},{4,12},{5,13},{6,14},{7,15},{8,11},{9,10},... | collective-permute-start | bytes 196616 | tf_op jit(solution)/shard_map/diag/ppermute | solution.py:56
  6.4 0.0 collective-permute-start.1
  6.4 2.1 %collective-permute-start = (f32[128,128]{1,0:T(8,128)S(1)}, f32[128,128]{1,0:T(8,128)S(1)}, u32[]{:S(2)}, u32[]{:S(2)}) collective-permute-start(f32[128,128]{1,0:T(8,128)S(1)} %slice.3), channel_id=1, source_target_pairs={{0,7},{1,6},{2,10},{3,11},{4,12},{5,13},{6,1},{7,0},{8,15},{9,14},... | collective-permute-start | bytes 196616 | tf_op jit(solution)/shard_map/diag/ppermute | solution.py:56
  8.5 0.0 collective-permute-done.2
  8.5 1.0 %collective-permute-done.1 = f32[128,128]{1,0:T(8,128)S(1)} collective-permute-done((f32[128,128]{1,0:T(8,128)S(1)}, f32[128,128]{1,0:T(8,128)S(1)}, u32[]{:S(2)}, u32[]{:S(2)}) %collective-permute-start.1) | collective-permute-done | bytes 65568 | tf_op jit(solution)/shard_map/diag/ppermute | solution.py:56
  9.5 2.2 %collective-permute-done = f32[128,128]{1,0:T(8,128)S(1)} collective-permute-done((f32[128,128]{1,0:T(8,128)S(1)}, f32[128,128]{1,0:T(8,128)S(1)}, u32[]{:S(2)}, u32[]{:S(2)}) %collective-permute-start) | collective-permute-done | bytes 65568 | tf_op jit(solution)/shard_map/diag/ppermute | solution.py:56
  11.8 0.1 collective-permute-start.5
  11.9 0.1 collective-permute-start.4
  12.0 0.1 collective-permute-start.3
  12.1 0.1 collective-permute-start.9
  12.2 3.6 %collective-permute-start.12 = (f32[128,128]{1,0:T(8,128)S(1)}, f32[128,128]{1,0:T(8,128)S(1)}, u32[]{:S(2)}, u32[]{:S(2)}) collective-permute-start(f32[128,128]{1,0:T(8,128)S(1)} %get-tuple-element.20), channel_id=1, source_target_pairs={{0,48},{1,56},{2,16},{3,24},{4,12},{5,13},{6,14},{7,15},{8,49},{9,... | collective-permute-start | bytes 196616 | tf_op jit(solution)/shard_map/cols/ppermute | solution.py:56
  15.8 0.0 collective-permute-done.5
  15.8 4.0 %collective-permute-start.13 = (f32[128,128]{1,0:T(8,128)S(1)}, f32[128,128]{1,0:T(8,128)S(1)}, u32[]{:S(2)}, u32[]{:S(2)}) collective-permute-start(f32[128,128]{1,0:T(8,128)S(1)} %get-tuple-element.21), channel_id=1, source_target_pairs={{0,32},{1,40},{2,10},{3,11},{4,0},{5,1},{6,14},{7,15},{8,33},{9,41... | collective-permute-start | bytes 196616 | tf_op jit(solution)/shard_map/cols/ppermute | solution.py:56
  19.8 1.9 %collective-permute-start.15 = (f32[128,128]{1,0:T(8,128)S(1)}, f32[128,128]{1,0:T(8,128)S(1)}, u32[]{:S(2)}, u32[]{:S(2)}) collective-permute-start(f32[128,128]{1,0:T(8,128)S(1)} %get-tuple-element.23), channel_id=1, source_target_pairs={{0,0},{1,8},{2,10},{3,11},{4,12},{5,13},{6,14},{7,15},{8,1},{9,9},... | collective-permute-start | bytes 196616 | tf_op jit(solution)/shard_map/cols/ppermute | solution.py:56
  21.7 0.1 collective-permute-start.8
  21.9 0.9 %collective-permute-start.7 = (f32[128,128]{1,0:T(8,128)S(1)}, f32[128,128]{1,0:T(8,128)S(1)}, u32[]{:S(2)}, u32[]{:S(2)}) collective-permute-start(f32[128,128]{1,0:T(8,128)S(1)} %select_select_fusion.2), channel_id=1, source_target_pairs={{0,192},{1,193},{2,194},{3,195},{4,196},{5,197},{6,198},{7,199},{8... | collective-permute-start | bytes 196616 | tf_op jit(solution)/shard_map/diag/ppermute | solution.py:56
  22.8 1.4 %collective-permute-start.6 = (f32[128,128]{1,0:T(8,128)S(1)}, f32[128,128]{1,0:T(8,128)S(1)}, u32[]{:S(2)}, u32[]{:S(2)}) collective-permute-start(f32[128,128]{1,0:T(8,128)S(1)} %select_select_fusion.2), channel_id=1, source_target_pairs={{0,128},{1,129},{2,130},{3,131},{4,132},{5,133},{6,134},{7,135},{8... | collective-permute-start | bytes 196616 | tf_op jit(solution)/shard_map/diag/ppermute | solution.py:56
  24.2 2.6 %collective-permute-done.14 = f32[128,128]{1,0:T(8,128)S(1)} collective-permute-done((f32[128,128]{1,0:T(8,128)S(1)}, f32[128,128]{1,0:T(8,128)S(1)}, u32[]{:S(2)}, u32[]{:S(2)}) %collective-permute-start.14) | collective-permute-done | bytes 65568 | tf_op jit(solution)/shard_map/cols/ppermute | solution.py:56
  26.8 0.0 collective-permute-done.15
  26.8 0.1 collective-permute-start.18
  26.9 1.1 %collective-permute-done.8 = f32[128,128]{1,0:T(8,128)S(1)} collective-permute-done((f32[128,128]{1,0:T(8,128)S(1)}, f32[128,128]{1,0:T(8,128)S(1)}, u32[]{:S(2)}, u32[]{:S(2)}) %collective-permute-start.8) | collective-permute-done | bytes 65568 | tf_op jit(solution)/shard_map/diag/ppermute | solution.py:56
  28.0 1.4 %collective-permute-start.17 = (f32[128,128]{1,0:T(8,128)S(1)}, f32[128,128]{1,0:T(8,128)S(1)}, u32[]{:S(2)}, u32[]{:S(2)}) collective-permute-start(f32[128,128]{1,0:T(8,128)S(1)} %select_select_fusion), channel_id=1, source_target_pairs={{0,128},{1,129},{2,130},{3,131},{4,132},{5,133},{6,134},{7,135},{8... | collective-permute-start | bytes 196616 | tf_op jit(solution)/shard_map/cols/ppermute | solution.py:56
  29.4 2.5 %collective-permute-start.16 = (f32[128,128]{1,0:T(8,128)S(1)}, f32[128,128]{1,0:T(8,128)S(1)}, u32[]{:S(2)}, u32[]{:S(2)}) collective-permute-start(f32[128,128]{1,0:T(8,128)S(1)} %select_select_fusion), channel_id=1, source_target_pairs={{0,192},{1,193},{2,194},{3,195},{4,196},{5,197},{6,198},{7,199},{8... | collective-permute-start | bytes 196616 | tf_op jit(solution)/shard_map/cols/ppermute | solution.py:56
  31.9 2.4 %collective-permute-done.10 = f32[512,128]{1,0:T(8,128)S(1)} collective-permute-done((f32[512,128]{1,0:T(8,128)S(1)}, f32[512,128]{1,0:T(8,128)S(1)}, u32[]{:S(2)}, u32[]{:S(2)}) %collective-permute-start.10) | collective-permute-done | bytes 262176 | tf_op jit(solution)/shard_map/rows/ppermute | solution.py:56
  34.3 0.7 %collective-permute-start.24 = (f32[128,128]{1,0:T(8,128)S(1)}, f32[128,128]{1,0:T(8,128)S(1)}, u32[]{:S(2)}, u32[]{:S(2)}) collective-permute-start(f32[128,128]{1,0:T(8,128)S(1)} %select_select_fusion.1.own_ref), channel_id=1, source_target_pairs={{0,9},{1,8},{2,11},{3,10},{4,13},{5,12},{6,15},{7,14},{8,1},{9,0},... | collective-permute-start | bytes 196616 | tf_op jit(solution)/shard_map/diag/ppermute | solution.py:56
  35.0 1.9 %collective-permute-start.23 = (f32[128,128]{1,0:T(8,128)S(1)}, f32[128,128]{1,0:T(8,128)S(1)}, u32[]{:S(2)}, u32[]{:S(2)}) collective-permute-start(f32[128,128]{1,0:T(8,128)S(1)} %select_select_fusion.1.own_ref), channel_id=1, source_target_pairs={{0,8},{1,9},{2,10},{3,11},{4,12},{5,13},{6,14},{7,15},{8,0},{9,1},... | collective-permute-start | bytes 196616 | tf_op jit(solution)/shard_map/diag/ppermute | solution.py:56
  36.9 0.0 collective-permute-done.18
  36.9 1.3 %collective-permute-start.22 = (f32[128,128]{1,0:T(8,128)S(1)}, f32[128,128]{1,0:T(8,128)S(1)}, u32[]{:S(2)}, u32[]{:S(2)}) collective-permute-start(f32[128,128]{1,0:T(8,128)S(1)} %select_select_fusion.1.own_ref), channel_id=1, source_target_pairs={{0,1},{1,0},{2,3},{3,2},{4,5},{5,4},{6,7},{7,6},{8,9},{9,8},{10,11... | collective-permute-start | bytes 196616 | tf_op jit(solution)/shard_map/diag/ppermute | solution.py:56
  38.2 0.0 collective-permute-done.16
  38.2 0.0 copy-start.1
  38.2 0.9 %collective-permute-start.25 = (f32[512,128]{1,0:T(8,128)S(1)}, f32[512,128]{1,0:T(8,128)S(1)}, u32[]{:S(2)}, u32[]{:S(2)}) collective-permute-start(f32[512,128]{1,0:T(8,128)S(1)} %pad_maximum_fusion.refs_0_), channel_id=1, source_target_pairs={{0,8},{1,9},{2,10},{3,11},{4,12},{5,13},{6,14},{7,15},{8,0},{9,1},... | collective-permute-start | bytes 786440 | tf_op jit(solution)/shard_map/cols/ppermute | solution.py:56
  39.1 2.2 %collective-permute-start.21 = (f32[512,128]{1,0:T(8,128)S(1)}, f32[512,128]{1,0:T(8,128)S(1)}, u32[]{:S(2)}, u32[]{:S(2)}) collective-permute-start(f32[512,128]{1,0:T(8,128)S(1)} %pad_maximum_fusion.refs_0_), channel_id=1, source_target_pairs={{0,16},{1,17},{2,18},{3,19},{4,20},{5,21},{6,22},{7,23},{8,24},{9,... | collective-permute-start | bytes 786440 | tf_op jit(solution)/shard_map/cols/ppermute | solution.py:56
  41.3 0.0 collective-permute-done.24.both_ref
  41.3 3.8 %collective-permute-start.20 = (f32[512,128]{1,0:T(8,128)S(1)}, f32[512,128]{1,0:T(8,128)S(1)}, u32[]{:S(2)}, u32[]{:S(2)}) collective-permute-start(f32[512,128]{1,0:T(8,128)S(1)} %pad_maximum_fusion.refs_0_), channel_id=1, source_target_pairs={{0,32},{1,33},{2,34},{3,35},{4,36},{5,37},{6,38},{7,39},{8,40},{9,... | collective-permute-start | bytes 786440 | tf_op jit(solution)/shard_map/cols/ppermute | solution.py:56
  45.1 0.1 collective-permute-start.19
  45.3 0.5 collective-permute-start.11
  45.7 8.3 %factorize.1 = (f32[256,256]{1,0:T(8,128)S(1)}, f32[256,256]{1,0:T(8,128)S(1)}) custom-call(s32[6]{0:T(128)S(1)} %stack.31.pos_ref, f32[128,128]{1,0:T(8,128)S(1)} %select_select_fusion.1.own_ref, f32[128,128]{1,0:T(8,128)S(1)} %collective-permute-done.22.across_ref, f32[128,128]{1,0:T(8,128)S(1)} %collective-permute-done.23.core_ref, ...), custom_call_target="tpu_custom_call" | custom-call | flops 4000000000 | bytes 800000 | tf_op jit(solution)/shard_map/diag/factorize/pallas_call | solution.py:175
  54.0 3.1 %collective-permute-done.20.refs_2_ = f32[512,128]{1,0:T(8,128)S(1)} collective-permute-done((f32[512,128]{1,0:T(8,128)S(1)}, f32[512,128]{1,0:T(8,128)S(1)}, u32[]{:S(2)}, u32[]{:S(2)}) %collective-permute-start.20) | collective-permute-done | bytes 262176 | tf_op jit(solution)/shard_map/cols/ppermute | solution.py:56
  57.1 0.9 %collective-permute-start.26 = (f32[512,128]{1,0:T(8,128)S(1)}, f32[512,128]{1,0:T(8,128)S(1)}, u32[]{:S(2)}, u32[]{:S(2)}) collective-permute-start(f32[512,128]{1,0:T(8,128)S(1)} %collective-permute-done.19.refs_1_), channel_id=1, source_target_pairs={{0,8},{1,9},{2,10},{3,11},{4,12},{5,13},{6,14},{7,15},{8,0},{9,1},... | collective-permute-start | bytes 786440 | tf_op jit(solution)/shard_map/cols/ppermute | solution.py:56
  58.0 0.0 collective-permute-start.27
  58.0 0.5 collective-permute-start.28
  58.5 0.6 collective-permute-done.26.refs_5_
  59.2 0.4 collective-permute-done.27.refs_6_
  59.6 0.4 collective-permute-done.28.refs_7_
  59.9 7.3 %update.1 = f32[8192,128]{1,0:T(8,128)} custom-call(s32[6]{0:T(128)S(1)} %stack.31.pos_ref, f32[8192,128]{1,0:T(8,128)S(1)} %bitcast.12, f32[512,128]{1,0:T(8,128)S(1)} %broadcast_select_fusion.1.near_ref, f32[512,128]{1,0:T(8,128)S(1)} %collective-permute-done.11.far_ref, f32[512,128]{1,0:T(8,128)S(1)} %pad_maximum_fusion.refs_0_, ...), custom_call_target="tpu_custom_call" | custom-call | flops 3000000000 | bytes 12000000 | tf_op jit(solution)/shard_map/final/update/pallas_call | solution.py:246
  (26 shorter events, 0.2 us)
Async XLA Ops:
  0.1 2.2 %copy-start = (f32[4,1,128,16,1,128]{5,4,3,2,1,0:T(1,128)S(1)}, f32[4,1,128,16,1,128]{5,4,3,2,1,0:T(1,128)}, u32[]{:S(2)}) copy-start(f32[4,1,128,16,1,128]{5,4,3,2,1,0:T(1,128)} %param.1) | copy-start | bytes 12582916
  3.0 5.5 %collective-permute-start.2 = (f32[128,128]{1,0:T(8,128)S(1)}, f32[128,128]{1,0:T(8,128)S(1)}, u32[]{:S(2)}, u32[]{:S(2)}) collective-permute-start(f32[128,128]{1,0:T(8,128)S(1)} %slice.3), channel_id=1, source_target_pairs={{0,3},{1,2},{2,1},{3,0},{4,12},{5,13},{6,14},{7,15},{8,11},{9,10},... | collective-permute-start | bytes 196616 | tf_op jit(solution)/shard_map/diag/ppermute | solution.py:56
  6.4 3.1 %collective-permute-start.1 = (f32[128,128]{1,0:T(8,128)S(1)}, f32[128,128]{1,0:T(8,128)S(1)}, u32[]{:S(2)}, u32[]{:S(2)}) collective-permute-start(f32[128,128]{1,0:T(8,128)S(1)} %slice.3), channel_id=1, source_target_pairs={{0,4},{1,5},{2,10},{3,11},{4,0},{5,1},{6,14},{7,15},{8,12},{9,13},... | collective-permute-start | bytes 196616 | tf_op jit(solution)/shard_map/diag/ppermute | solution.py:56
  6.4 5.3 %collective-permute-start = (f32[128,128]{1,0:T(8,128)S(1)}, f32[128,128]{1,0:T(8,128)S(1)}, u32[]{:S(2)}, u32[]{:S(2)}) collective-permute-start(f32[128,128]{1,0:T(8,128)S(1)} %slice.3), channel_id=1, source_target_pairs={{0,7},{1,6},{2,10},{3,11},{4,12},{5,13},{6,1},{7,0},{8,15},{9,14},... | collective-permute-start | bytes 196616 | tf_op jit(solution)/shard_map/diag/ppermute | solution.py:56
  11.8 4.0 %collective-permute-start.5 = (f32[128,128]{1,0:T(8,128)S(1)}, f32[128,128]{1,0:T(8,128)S(1)}, u32[]{:S(2)}, u32[]{:S(2)}) collective-permute-start(f32[128,128]{1,0:T(8,128)S(1)} %select_select_fusion.3), channel_id=1, source_target_pairs={{0,16},{1,17},{2,18},{3,19},{4,20},{5,21},{6,22},{7,23},{8,24},{9,... | collective-permute-start | bytes 196616 | tf_op jit(solution)/shard_map/diag/ppermute | solution.py:56
  11.9 7.9 %collective-permute-start.4 = (f32[128,128]{1,0:T(8,128)S(1)}, f32[128,128]{1,0:T(8,128)S(1)}, u32[]{:S(2)}, u32[]{:S(2)}) collective-permute-start(f32[128,128]{1,0:T(8,128)S(1)} %select_select_fusion.3), channel_id=1, source_target_pairs={{0,48},{1,49},{2,50},{3,51},{4,52},{5,53},{6,54},{7,55},{8,56},{9,... | collective-permute-start | bytes 196616 | tf_op jit(solution)/shard_map/diag/ppermute | solution.py:56
  12.0 7.8 %collective-permute-start.3 = (f32[128,128]{1,0:T(8,128)S(1)}, f32[128,128]{1,0:T(8,128)S(1)}, u32[]{:S(2)}, u32[]{:S(2)}) collective-permute-start(f32[128,128]{1,0:T(8,128)S(1)} %select_select_fusion.3), channel_id=1, source_target_pairs={{0,32},{1,33},{2,34},{3,35},{4,36},{5,37},{6,38},{7,39},{8,40},{9,... | collective-permute-start | bytes 196616 | tf_op jit(solution)/shard_map/diag/ppermute | solution.py:56
  12.1 9.7 %collective-permute-start.9 = (f32[512,128]{1,0:T(8,128)S(1)}, f32[512,128]{1,0:T(8,128)S(1)}, u32[]{:S(2)}, u32[]{:S(2)}) collective-permute-start(f32[512,128]{1,0:T(8,128)S(1)} %get-tuple-element.18), channel_id=1, source_target_pairs={{0,4},{1,5},{2,10},{3,11},{4,0},{5,1},{6,14},{7,15},{8,12},{9,13},... | collective-permute-start | bytes 786440 | tf_op jit(solution)/shard_map/rows/ppermute | solution.py:56
  12.2 9.7 %collective-permute-start.12 = (f32[128,128]{1,0:T(8,128)S(1)}, f32[128,128]{1,0:T(8,128)S(1)}, u32[]{:S(2)}, u32[]{:S(2)}) collective-permute-start(f32[128,128]{1,0:T(8,128)S(1)} %get-tuple-element.20), channel_id=1, source_target_pairs={{0,48},{1,56},{2,16},{3,24},{4,12},{5,13},{6,14},{7,15},{8,49},{9,... | collective-permute-start | bytes 196616 | tf_op jit(solution)/shard_map/cols/ppermute | solution.py:56
  15.8 7.0 %collective-permute-start.13 = (f32[128,128]{1,0:T(8,128)S(1)}, f32[128,128]{1,0:T(8,128)S(1)}, u32[]{:S(2)}, u32[]{:S(2)}) collective-permute-start(f32[128,128]{1,0:T(8,128)S(1)} %get-tuple-element.21), channel_id=1, source_target_pairs={{0,32},{1,40},{2,10},{3,11},{4,0},{5,1},{6,14},{7,15},{8,33},{9,41... | collective-permute-start | bytes 196616 | tf_op jit(solution)/shard_map/cols/ppermute | solution.py:56
  19.8 7.0 %collective-permute-start.14 = (f32[128,128]{1,0:T(8,128)S(1)}, f32[128,128]{1,0:T(8,128)S(1)}, u32[]{:S(2)}, u32[]{:S(2)}) collective-permute-start(f32[128,128]{1,0:T(8,128)S(1)} %get-tuple-element.22), channel_id=1, source_target_pairs={{0,16},{1,24},{2,10},{3,11},{4,12},{5,13},{6,48},{7,56},{8,17},{9,... | collective-permute-start | bytes 196616 | tf_op jit(solution)/shard_map/cols/ppermute | solution.py:56
  19.8 7.0 %collective-permute-start.15 = (f32[128,128]{1,0:T(8,128)S(1)}, f32[128,128]{1,0:T(8,128)S(1)}, u32[]{:S(2)}, u32[]{:S(2)}) collective-permute-start(f32[128,128]{1,0:T(8,128)S(1)} %get-tuple-element.23), channel_id=1, source_target_pairs={{0,0},{1,8},{2,10},{3,11},{4,12},{5,13},{6,14},{7,15},{8,1},{9,9},... | collective-permute-start | bytes 196616 | tf_op jit(solution)/shard_map/cols/ppermute | solution.py:56
  21.7 6.3 %collective-permute-start.8 = (f32[128,128]{1,0:T(8,128)S(1)}, f32[128,128]{1,0:T(8,128)S(1)}, u32[]{:S(2)}, u32[]{:S(2)}) collective-permute-start(f32[128,128]{1,0:T(8,128)S(1)} %select_select_fusion.2), channel_id=1, source_target_pairs={{0,64},{1,65},{2,66},{3,67},{4,68},{5,69},{6,70},{7,71},{8,72},{9,... | collective-permute-start | bytes 196616 | tf_op jit(solution)/shard_map/diag/ppermute | solution.py:56
  21.9 7.5 %collective-permute-start.7 = (f32[128,128]{1,0:T(8,128)S(1)}, f32[128,128]{1,0:T(8,128)S(1)}, u32[]{:S(2)}, u32[]{:S(2)}) collective-permute-start(f32[128,128]{1,0:T(8,128)S(1)} %select_select_fusion.2), channel_id=1, source_target_pairs={{0,192},{1,193},{2,194},{3,195},{4,196},{5,197},{6,198},{7,199},{8... | collective-permute-start | bytes 196616 | tf_op jit(solution)/shard_map/diag/ppermute | solution.py:56
  22.8 9.1 %collective-permute-start.6 = (f32[128,128]{1,0:T(8,128)S(1)}, f32[128,128]{1,0:T(8,128)S(1)}, u32[]{:S(2)}, u32[]{:S(2)}) collective-permute-start(f32[128,128]{1,0:T(8,128)S(1)} %select_select_fusion.2), channel_id=1, source_target_pairs={{0,128},{1,129},{2,130},{3,131},{4,132},{5,133},{6,134},{7,135},{8... | collective-permute-start | bytes 196616 | tf_op jit(solution)/shard_map/diag/ppermute | solution.py:56
  26.8 7.5 %collective-permute-start.10 = (f32[512,128]{1,0:T(8,128)S(1)}, f32[512,128]{1,0:T(8,128)S(1)}, u32[]{:S(2)}, u32[]{:S(2)}) collective-permute-start(f32[512,128]{1,0:T(8,128)S(1)} %broadcast_select_fusion), channel_id=1, source_target_pairs={{0,3},{1,2},{2,1},{3,0},{4,7},{5,6},{6,5},{7,4},{8,11},{9,10},{10,... | collective-permute-start | bytes 786440 | tf_op jit(solution)/shard_map/rows/ppermute | solution.py:56
  26.8 10.1 %collective-permute-start.18 = (f32[128,128]{1,0:T(8,128)S(1)}, f32[128,128]{1,0:T(8,128)S(1)}, u32[]{:S(2)}, u32[]{:S(2)}) collective-permute-start(f32[128,128]{1,0:T(8,128)S(1)} %select_select_fusion), channel_id=1, source_target_pairs={{0,64},{1,65},{2,66},{3,67},{4,68},{5,69},{6,70},{7,71},{8,72},{9,... | collective-permute-start | bytes 196616 | tf_op jit(solution)/shard_map/cols/ppermute | solution.py:56
  28.0 10.2 %collective-permute-start.17 = (f32[128,128]{1,0:T(8,128)S(1)}, f32[128,128]{1,0:T(8,128)S(1)}, u32[]{:S(2)}, u32[]{:S(2)}) collective-permute-start(f32[128,128]{1,0:T(8,128)S(1)} %select_select_fusion), channel_id=1, source_target_pairs={{0,128},{1,129},{2,130},{3,131},{4,132},{5,133},{6,134},{7,135},{8... | collective-permute-start | bytes 196616 | tf_op jit(solution)/shard_map/cols/ppermute | solution.py:56
  29.4 8.8 %collective-permute-start.16 = (f32[128,128]{1,0:T(8,128)S(1)}, f32[128,128]{1,0:T(8,128)S(1)}, u32[]{:S(2)}, u32[]{:S(2)}) collective-permute-start(f32[128,128]{1,0:T(8,128)S(1)} %select_select_fusion), channel_id=1, source_target_pairs={{0,192},{1,193},{2,194},{3,195},{4,196},{5,197},{6,198},{7,199},{8... | collective-permute-start | bytes 196616 | tf_op jit(solution)/shard_map/cols/ppermute | solution.py:56
  34.3 7.0 %collective-permute-start.24 = (f32[128,128]{1,0:T(8,128)S(1)}, f32[128,128]{1,0:T(8,128)S(1)}, u32[]{:S(2)}, u32[]{:S(2)}) collective-permute-start(f32[128,128]{1,0:T(8,128)S(1)} %select_select_fusion.1.own_ref), channel_id=1, source_target_pairs={{0,9},{1,8},{2,11},{3,10},{4,13},{5,12},{6,15},{7,14},{8,1},{9,0},... | collective-permute-start | bytes 196616 | tf_op jit(solution)/shard_map/diag/ppermute | solution.py:56
  35.0 10.2 %collective-permute-start.23 = (f32[128,128]{1,0:T(8,128)S(1)}, f32[128,128]{1,0:T(8,128)S(1)}, u32[]{:S(2)}, u32[]{:S(2)}) collective-permute-start(f32[128,128]{1,0:T(8,128)S(1)} %select_select_fusion.1.own_ref), channel_id=1, source_target_pairs={{0,8},{1,9},{2,10},{3,11},{4,12},{5,13},{6,14},{7,15},{8,0},{9,1},... | collective-permute-start | bytes 196616 | tf_op jit(solution)/shard_map/diag/ppermute | solution.py:56
  36.9 8.3 %collective-permute-start.22 = (f32[128,128]{1,0:T(8,128)S(1)}, f32[128,128]{1,0:T(8,128)S(1)}, u32[]{:S(2)}, u32[]{:S(2)}) collective-permute-start(f32[128,128]{1,0:T(8,128)S(1)} %select_select_fusion.1.own_ref), channel_id=1, source_target_pairs={{0,1},{1,0},{2,3},{3,2},{4,5},{5,4},{6,7},{7,6},{8,9},{9,8},{10,11... | collective-permute-start | bytes 196616 | tf_op jit(solution)/shard_map/diag/ppermute | solution.py:56
  38.2 21.7 %copy-start.1 = (f32[4,1,128,16,1,128]{5,4,3,2,1,0:T(1,128)S(1)}, f32[4,1,128,16,1,128]{5,4,3,2,1,0:T(1,128)}, u32[]{:S(2)}) copy-start(f32[4,1,128,16,1,128]{5,4,3,2,1,0:T(1,128)} %param.1) | copy-start | bytes 12582916
  38.2 20.3 %collective-permute-start.25 = (f32[512,128]{1,0:T(8,128)S(1)}, f32[512,128]{1,0:T(8,128)S(1)}, u32[]{:S(2)}, u32[]{:S(2)}) collective-permute-start(f32[512,128]{1,0:T(8,128)S(1)} %pad_maximum_fusion.refs_0_), channel_id=1, source_target_pairs={{0,8},{1,9},{2,10},{3,11},{4,12},{5,13},{6,14},{7,15},{8,0},{9,1},... | collective-permute-start | bytes 786440 | tf_op jit(solution)/shard_map/cols/ppermute | solution.py:56
  39.1 14.9 %collective-permute-start.21 = (f32[512,128]{1,0:T(8,128)S(1)}, f32[512,128]{1,0:T(8,128)S(1)}, u32[]{:S(2)}, u32[]{:S(2)}) collective-permute-start(f32[512,128]{1,0:T(8,128)S(1)} %pad_maximum_fusion.refs_0_), channel_id=1, source_target_pairs={{0,16},{1,17},{2,18},{3,19},{4,20},{5,21},{6,22},{7,23},{8,24},{9,... | collective-permute-start | bytes 786440 | tf_op jit(solution)/shard_map/cols/ppermute | solution.py:56
  41.3 15.8 %collective-permute-start.20 = (f32[512,128]{1,0:T(8,128)S(1)}, f32[512,128]{1,0:T(8,128)S(1)}, u32[]{:S(2)}, u32[]{:S(2)}) collective-permute-start(f32[512,128]{1,0:T(8,128)S(1)} %pad_maximum_fusion.refs_0_), channel_id=1, source_target_pairs={{0,32},{1,33},{2,34},{3,35},{4,36},{5,37},{6,38},{7,39},{8,40},{9,... | collective-permute-start | bytes 786440 | tf_op jit(solution)/shard_map/cols/ppermute | solution.py:56
  45.1 12.0 %collective-permute-start.19 = (f32[512,128]{1,0:T(8,128)S(1)}, f32[512,128]{1,0:T(8,128)S(1)}, u32[]{:S(2)}, u32[]{:S(2)}) collective-permute-start(f32[512,128]{1,0:T(8,128)S(1)} %pad_maximum_fusion.refs_0_), channel_id=1, source_target_pairs={{0,48},{1,49},{2,50},{3,51},{4,52},{5,53},{6,54},{7,55},{8,56},{9,... | collective-permute-start | bytes 786440 | tf_op jit(solution)/shard_map/cols/ppermute | solution.py:56
  45.3 13.3 %collective-permute-start.11 = (f32[512,128]{1,0:T(8,128)S(1)}, f32[512,128]{1,0:T(8,128)S(1)}, u32[]{:S(2)}, u32[]{:S(2)}) collective-permute-start(f32[512,128]{1,0:T(8,128)S(1)} %broadcast_select_fusion.1.near_ref), channel_id=1, source_target_pairs={{0,1},{1,0},{2,3},{3,2},{4,5},{5,4},{6,7},{7,6},{8,9},{9,8},{10,11... | collective-permute-start | bytes 786440 | tf_op jit(solution)/shard_map/diag/ppermute | solution.py:56
  57.1 2.0 %collective-permute-start.26 = (f32[512,128]{1,0:T(8,128)S(1)}, f32[512,128]{1,0:T(8,128)S(1)}, u32[]{:S(2)}, u32[]{:S(2)}) collective-permute-start(f32[512,128]{1,0:T(8,128)S(1)} %collective-permute-done.19.refs_1_), channel_id=1, source_target_pairs={{0,8},{1,9},{2,10},{3,11},{4,12},{5,13},{6,14},{7,15},{8,0},{9,1},... | collective-permute-start | bytes 786440 | tf_op jit(solution)/shard_map/cols/ppermute | solution.py:56
  58.0 1.5 %collective-permute-start.27 = (f32[512,128]{1,0:T(8,128)S(1)}, f32[512,128]{1,0:T(8,128)S(1)}, u32[]{:S(2)}, u32[]{:S(2)}) collective-permute-start(f32[512,128]{1,0:T(8,128)S(1)} %collective-permute-done.20.refs_2_), channel_id=1, source_target_pairs={{0,8},{1,9},{2,10},{3,11},{4,12},{5,13},{6,14},{7,15},{8,0},{9,1},... | collective-permute-start | bytes 786440 | tf_op jit(solution)/shard_map/cols/ppermute | solution.py:56
  58.0 1.9 %collective-permute-start.28 = (f32[512,128]{1,0:T(8,128)S(1)}, f32[512,128]{1,0:T(8,128)S(1)}, u32[]{:S(2)}, u32[]{:S(2)}) collective-permute-start(f32[512,128]{1,0:T(8,128)S(1)} %collective-permute-done.21.refs_3_), channel_id=1, source_target_pairs={{0,8},{1,9},{2,10},{3,11},{4,12},{5,13},{6,14},{7,15},{8,0},{9,1},... | collective-permute-start | bytes 786440 | tf_op jit(solution)/shard_map/cols/ppermute | solution.py:56

commit v3 on v2

--- a/solution.py
+++ b/solution.py
@@ -185,25 +185,69 @@
     )(pos, own, across, core, both)
 
 
-def update_kernel(rows, pos_ref, a_ref, near_ref, far_ref, *refs):
-    mine = refs[0:4]
-    other = refs[4:8]
-    w_ref, u_ref, o_ref = refs[8:11]
-    thigh_ref, tlow_ref, shigh_ref, slow_ref, top_ref, left_ref, sum_ref = refs[11:]
+def early_kernel(pos_ref, near_ref, far_ref, mine_ref, other_ref, w_ref, s_ref, t_ref):
+    even, low = pos_ref[4] == 0, pos_ref[5] == 1
+    wlo, whi = w_ref[:, :BLK], w_ref[:, BLK:]
+    wnear, wfar = jnp.where(low, wlo, whi), jnp.where(low, whi, wlo)
+    s_ref[...] = dot_pairs([(near_ref[...], wnear), (far_ref[...], wfar)])
+    wmine, wother = jnp.where(even, wlo, whi), jnp.where(even, whi, wlo)
+    t_ref[...] = dot_pairs([(wmine, mine_ref[...]), (wother, other_ref[...])])
+
+
+def solve_early(pos, near, far, mine, other, inverse):
+    vmem = pl.BlockSpec(memory_space=pltpu.VMEM)
+    return pl.pallas_call(
+        early_kernel,
+        out_shape=[
+            jax.ShapeDtypeStruct((512, PANEL), jnp.float32),
+            jax.ShapeDtypeStruct((PANEL, 512), jnp.float32),
+        ],
+        in_specs=[pl.BlockSpec(memory_space=pltpu.SMEM)] + [vmem] * 5,
+        out_specs=[vmem] * 2,
+        compiler_params=pltpu.CompilerParams(vmem_limit_bytes=24 * 1024 * 1024),
+        cost_estimate=pl.CostEstimate(flops=1000000000, bytes_accessed=3000000, transcendentals=0),
+        name="solve_early",
+    )(pos, near, far, mine, other, inverse)
+
+
+def sides_kernel(pos_ref, up_ref, up_other_ref, down_ref, down_other_ref, w_ref, up_t_ref, down_t_ref):
+    even = pos_ref[4] == 0
+    wlo, whi = w_ref[:, :BLK], w_ref[:, BLK:]
+    wmine, wother = jnp.where(even, wlo, whi), jnp.where(even, whi, wlo)
+    up_t_ref[...] = dot_pairs([(wmine, up_ref[...]), (wother, up_other_ref[...])])
+    down_t_ref[...] = dot_pairs([(wmine, down_ref[...]), (wother, down_other_ref[...])])
+
+
+def solve_sides(pos, up, up_other, down, down_other, inverse):
+    vmem = pl.BlockSpec(memory_space=pltpu.VMEM)
+    return pl.pallas_call(
+        sides_kernel,
+        out_shape=[jax.ShapeDtypeStruct((PANEL, 512), jnp.float32)] * 2,
+        in_specs=[pl.BlockSpec(memory_space=pltpu.SMEM)] + [vmem] * 5,
+        out_specs=[vmem] * 2,
+        compiler_params=pltpu.CompilerParams(vmem_limit_bytes=24 * 1024 * 1024),
+        cost_estimate=pl.CostEstimate(flops=1000000000, bytes_accessed=3000000, transcendentals=0),
+        name="solve_sides",
+    )(pos, up, up_other, down, down_other, inverse)
+
+
+def update_kernel(rows, pos_ref, a_ref, *refs):
+    s_ref, own_ref, up_ref, down_ref, mine_ref, other_ref = refs[0:6]
+    w_ref, u_ref, o_ref = refs[6:9]
+    thigh_ref, tlow_ref, top_ref, sum_ref = refs[9:]
     step = pl.program_id(0)
     row, col, y, zh = pos_ref[0], pos_ref[1], pos_ref[2], pos_ref[3]
-    even, low = pos_ref[4] == 0, pos_ref[5] == 1
+    even = pos_ref[4] == 0
 
     @pl.when(step == 0)
     def _():
         wlo, whi = w_ref[:, :BLK], w_ref[:, BLK:]
-        wnear, wfar = jnp.where(low, wlo, whi), jnp.where(low, whi, wlo)
-        solved = dot_pairs([(near_ref[...], wnear), (far_ref[...], wfar)])
-        shigh_ref[...], slow_ref[...] = halves(solved)
-        left_ref[...] = jnp.where(col == 0, solved[:, :BLK], solved[:, BLK:])
         wmine, wother = jnp.where(even, wlo, whi), jnp.where(even, whi, wlo)
         for d in range(4):
-            solved = dot_pairs([(wmine, mine[d][...]), (wother, other[d][...])])
+            if d == 2:
+                solved = dot_pairs([(wmine, mine_ref[...]), (wother, other_ref[...])])
+            else:
+                solved = (own_ref, up_ref, None, down_ref)[d][...]
             high, lower = halves(solved)
             for k in range(4):
                 j = 4 * lax.rem(y + d, 4) + lax.rem(zh + k, 4)
@@ -217,7 +261,8 @@
                     top_ref[:, at] = jnp.where(row == 0, block[:BLK], block[BLK:])
 
     at = pl.ds(pl.multiple_of(step * rows, rows), rows)
-    shigh, slow = shigh_ref[at, :], slow_ref[at, :]
+    solved_rows = s_ref[at, :]
+    shigh, slow = halves(solved_rows)
     wide = jnp.concatenate([shigh, shigh, slow], 1)
     for n in range(8):
         cut = slice(n * 256, (n + 1) * 256)
@@ -231,7 +276,9 @@
 
     @pl.when(col < 2)
     def _():
-        o_ref[pl.ds(0, rows, 16), :] = left_ref[at, :]
+        o_ref[pl.ds(0, rows, 16), :] = jnp.where(
+            col == 0, solved_rows[:, :BLK], solved_rows[:, BLK:]
+        )
 
     @pl.when((row < 2) & (col < 2) & (step == 0))
     def _():
@@ -239,7 +286,7 @@
         o_ref[pl.ds(0, BLK, 16), :] = jnp.where(row == 0, strip[:, :BLK], strip[:, BLK:]).T
 
 
-def update(pos, a, near, far, mine, other, inverse, upper):
+def update(pos, a, early, mine, other, inverse, upper):
     rows = 2 * BLK
     vmem = pl.BlockSpec(memory_space=pltpu.VMEM)
     tile = pl.BlockSpec((rows * 16, BLK), lambda i: (i, 0))
@@ -247,15 +294,12 @@
         functools.partial(update_kernel, rows),
         grid=(512 // rows,),
         out_shape=jax.ShapeDtypeStruct(a.shape, jnp.float32),
-        in_specs=[pl.BlockSpec(memory_space=pltpu.SMEM), tile] + [vmem] * 12,
+        in_specs=[pl.BlockSpec(memory_space=pltpu.SMEM), tile] + [vmem] * 8,
         out_specs=tile,
         scratch_shapes=[
             pltpu.VMEM((PANEL, 2048), jnp.bfloat16),
             pltpu.VMEM((PANEL, 2048), jnp.bfloat16),
-            pltpu.VMEM((512, PANEL), jnp.bfloat16),
-            pltpu.VMEM((512, PANEL), jnp.bfloat16),
             pltpu.VMEM((BLK, 2048), jnp.float32),
-            pltpu.VMEM((512, BLK), jnp.float32),
             pltpu.VMEM((rows, 2048), jnp.float32),
         ],
         compiler_params=pltpu.CompilerParams(vmem_limit_bytes=40 * 1024 * 1024),
@@ -263,7 +307,7 @@
             flops=3000000000, bytes_accessed=12000000, transcendentals=0
         ),
         name="update",
-    )(pos, a, near, far, *mine, *other, inverse, upper)
+    )(pos, a, *early, mine, other, inverse, upper)
 
 
 def local(kernel):
@@ -328,15 +372,23 @@
             send(piece, lambda zh, y, core, zl, x, s=s: (zh - s, y, core, zl, x)) for s in (1, 2, 3)
         ]
         own = jnp.concatenate(over_z)
+        halfway = send(own, lambda zh, y, core, zl, x: (zh, y - 2, core, zl, x))
         around = [
-            send(own, lambda zh, y, core, zl, x, s=s: (zh, y - s, core, zl, x)) for s in (1, 2, 3)
-        ]
-        *around, inverse = lax.optimization_barrier((*around, inverse))
-        mine = [own] + around
-        other = [send(v, lambda zh, y, core, zl, x: (zh, y, 1 - core, zl, x)) for v in mine]
+            send(own, lambda zh, y, core, zl, x: (zh, y - 1, core, zl, x)),
+            halfway,
+            send(own, lambda zh, y, core, zl, x: (zh, y - 3, core, zl, x)),
+        ]
+        swap = lambda zh, y, core, zl, x: (zh, y, 1 - core, zl, x)
+        own_other = send(own, swap)
+        up, down, inverse = lax.optimization_barrier((around[0], around[2], inverse))
+        other = [own_other, send(up, swap), None, send(down, swap)]
+        early = solve_early(pos, near, far, own, own_other, inverse)
+        opposite, *early = lax.optimization_barrier((around[1], *early))
+        other[2] = send(opposite, swap)
+        sides = solve_sides(pos, up, other[1], down, other[3], inverse)
 
     with jax.named_scope("final"):
-        out = update(pos, flat, near, far, mine, other, inverse, upper)
+        out = update(pos, flat, [*early, *sides], opposite, other[2], inverse, upper)
     return out.reshape(kernel.shape)
 
 

time: 67.3 us -> 64.8 us (0.963)
  waiting for transfers between devices: 13.9 us -> 9.35 us
  Pallas kernels: 16.3 us -> 17.5 us
  starting transfers between devices: 34.5 us -> 35.2 us
    ppermute x29, waiting for transfers between devices: 13.9 us -> 9.35 us  [send(): return lax.ppermute(value, AXES, closed(pairs_of(target)))]
    pallas_call x0 -> x2, Pallas kernels: none -> 2.32 us  [the longest x1 1.17 us: solve_early(): pl.pallas_call(early_kernel, out_shape=[jax.ShapeDtypeStruct((512, PANEL)...]
    pallas_call x1, Pallas kernels: 7.27 us -> 6.15 us  [update(): pl.pallas_call(functools.partial(update_kernel, rows), grid=(512 // rows,...]
    ppermute x29, starting transfers between devices: 34.5 us -> 35.2 us  [send(): return lax.ppermute(value, AXES, closed(pairs_of(target)))]
  transfers between devices with their start and end apart: 29 -> 29, of which waited for: 9 -> 5; matrix products, arithmetic and copies ran while one was open for 0% -> 0% of each run, Pallas kernels for 12% -> 16%
where the time goes in v3:
time: 64.8 us; the launch traced here: 64.7 us
  starting transfers between devices  35.2 us (54%)
  Pallas kernels  17.5 us (27%)
  waiting for transfers between devices  9.35 us (14%)
  local copies, waits for them, and re-layouts  2.28 us (4%)
    ppermute x29, starting transfers between devices, send(): return lax.ppermute(value, AXES, closed(pairs_of(target)))  35.2 us
    ppermute x29, waiting for transfers between devices, send(): return lax.ppermute(value, AXES, closed(pairs_of(target)))  9.35 us
    pallas_call x1, Pallas kernels, factorize(): pl.pallas_call(functools.partial(factor_kernel, 32), out_shape=[square, s...  8.27 us
    pallas_call x1, Pallas kernels, update(): pl.pallas_call(functools.partial(update_kernel, rows), grid=(512 // rows,...  6.15 us
    unnamed x4, local copies, waits for them, and re-layouts  2.2 us
  transfers between devices with their start and end apart: 29, of which 5 were waited for; matrix products, arithmetic and copies ran while one was open for 0% of the time, Pallas kernels for 16%

profile of v3, /device:TPU:1, one launch (start us, length us, event | category | flops | bytes accessed | tf_op | source)
XLA Modules:
  0.0 64.7 jit_solution(5805510775606769876)
XLA Ops:
  0.0 0.1 stack.31.pos_ref
  0.1 2.2 %copy-done = f32[4,1,128,16,1,128]{5,4,3,2,1,0:T(1,128)S(1)} copy-done((f32[4,1,128,16,1,128]{5,4,3,2,1,0:T(1,128)S(1)}, f32[4,1,128,16,1,128]{5,4,3,2,1,0:T(1,128)}, u32[]{:S(2)}) %copy-start) | copy-done | bytes 4194328
  2.3 0.7 %prepare.1 = (f32[512,128]{1,0:T(8,128)S(1)}, f32[128,128]{1,0:T(8,128)S(1)}, f32[128,128]{1,0:T(8,128)S(1)}, f32[128,128]{1,0:T(8,128)S(1)}, f32[128,128]{1,0:T(8,128)S(1)}) custom-call(s32[6]{0:T(128)S(1)} %stack.31.pos_ref, f32[512,16,128]{2,1,0:T(8,128)S(1)} %bitcast.11), custom_call_target="tpu_custom_call" | custom-call | tf_op jit(solution)/shard_map/prepare/pallas_call | solution.py:102
  3.0 3.4 %collective-permute-start.10 = (f32[128,128]{1,0:T(8,128)S(1)}, f32[128,128]{1,0:T(8,128)S(1)}, u32[]{:S(2)}, u32[]{:S(2)}) collective-permute-start(f32[128,128]{1,0:T(8,128)S(1)} %slice.3), channel_id=1, source_target_pairs={{0,3},{1,2},{2,1},{3,0},{4,12},{5,13},{6,14},{7,15},{8,11},{9,10},... | collective-permute-start | bytes 196616 | tf_op jit(solution)/shard_map/diag/ppermute | solution.py:56
  6.4 0.0 collective-permute-start.9
  6.4 2.1 %collective-permute-start.8 = (f32[128,128]{1,0:T(8,128)S(1)}, f32[128,128]{1,0:T(8,128)S(1)}, u32[]{:S(2)}, u32[]{:S(2)}) collective-permute-start(f32[128,128]{1,0:T(8,128)S(1)} %slice.3), channel_id=1, source_target_pairs={{0,7},{1,6},{2,10},{3,11},{4,12},{5,13},{6,1},{7,0},{8,15},{9,14},... | collective-permute-start | bytes 196616 | tf_op jit(solution)/shard_map/diag/ppermute | solution.py:56
  8.5 0.0 collective-permute-done.10
  8.5 1.0 %collective-permute-done.9 = f32[128,128]{1,0:T(8,128)S(1)} collective-permute-done((f32[128,128]{1,0:T(8,128)S(1)}, f32[128,128]{1,0:T(8,128)S(1)}, u32[]{:S(2)}, u32[]{:S(2)}) %collective-permute-start.9) | collective-permute-done | bytes 65568 | tf_op jit(solution)/shard_map/diag/ppermute | solution.py:56
  9.5 2.2 %collective-permute-done.8 = f32[128,128]{1,0:T(8,128)S(1)} collective-permute-done((f32[128,128]{1,0:T(8,128)S(1)}, f32[128,128]{1,0:T(8,128)S(1)}, u32[]{:S(2)}, u32[]{:S(2)}) %collective-permute-start.8) | collective-permute-done | bytes 65568 | tf_op jit(solution)/shard_map/diag/ppermute | solution.py:56
  11.8 0.1 collective-permute-start.13
  11.9 0.1 collective-permute-start.12
  12.0 0.1 collective-permute-start.11
  12.1 0.1 collective-permute-start.17
  12.2 3.6 %collective-permute-start = (f32[128,128]{1,0:T(8,128)S(1)}, f32[128,128]{1,0:T(8,128)S(1)}, u32[]{:S(2)}, u32[]{:S(2)}) collective-permute-start(f32[128,128]{1,0:T(8,128)S(1)} %get-tuple-element.24), channel_id=1, source_target_pairs={{0,48},{1,56},{2,16},{3,24},{4,12},{5,13},{6,14},{7,15},{8,49},{9,... | collective-permute-start | bytes 196616 | tf_op jit(solution)/shard_map/cols/ppermute | solution.py:56
  15.8 0.0 collective-permute-done.13
  15.8 4.0 %collective-permute-start.1 = (f32[128,128]{1,0:T(8,128)S(1)}, f32[128,128]{1,0:T(8,128)S(1)}, u32[]{:S(2)}, u32[]{:S(2)}) collective-permute-start(f32[128,128]{1,0:T(8,128)S(1)} %get-tuple-element.25), channel_id=1, source_target_pairs={{0,32},{1,40},{2,10},{3,11},{4,0},{5,1},{6,14},{7,15},{8,33},{9,41... | collective-permute-start | bytes 196616 | tf_op jit(solution)/shard_map/cols/ppermute | solution.py:56
  19.7 0.0 collective-permute-done.12
  19.8 1.9 %collective-permute-start.3 = (f32[128,128]{1,0:T(8,128)S(1)}, f32[128,128]{1,0:T(8,128)S(1)}, u32[]{:S(2)}, u32[]{:S(2)}) collective-permute-start(f32[128,128]{1,0:T(8,128)S(1)} %get-tuple-element.27), channel_id=1, source_target_pairs={{0,0},{1,8},{2,10},{3,11},{4,12},{5,13},{6,14},{7,15},{8,1},{9,9},... | collective-permute-start | bytes 196616 | tf_op jit(solution)/shard_map/cols/ppermute | solution.py:56
  21.7 0.1 collective-permute-start.16
  21.9 0.9 %collective-permute-start.15 = (f32[128,128]{1,0:T(8,128)S(1)}, f32[128,128]{1,0:T(8,128)S(1)}, u32[]{:S(2)}, u32[]{:S(2)}) collective-permute-start(f32[128,128]{1,0:T(8,128)S(1)} %select_select_fusion.1), channel_id=1, source_target_pairs={{0,192},{1,193},{2,194},{3,195},{4,196},{5,197},{6,198},{7,199},{8... | collective-permute-start | bytes 196616 | tf_op jit(solution)/shard_map/diag/ppermute | solution.py:56
  22.8 0.0 collective-permute-done.1
  22.8 1.4 %collective-permute-start.14 = (f32[128,128]{1,0:T(8,128)S(1)}, f32[128,128]{1,0:T(8,128)S(1)}, u32[]{:S(2)}, u32[]{:S(2)}) collective-permute-start(f32[128,128]{1,0:T(8,128)S(1)} %select_select_fusion.1), channel_id=1, source_target_pairs={{0,128},{1,129},{2,130},{3,131},{4,132},{5,133},{6,134},{7,135},{8... | collective-permute-start | bytes 196616 | tf_op jit(solution)/shard_map/diag/ppermute | solution.py:56
  24.2 2.6 %collective-permute-done.2 = f32[128,128]{1,0:T(8,128)S(1)} collective-permute-done((f32[128,128]{1,0:T(8,128)S(1)}, f32[128,128]{1,0:T(8,128)S(1)}, u32[]{:S(2)}, u32[]{:S(2)}) %collective-permute-start.2) | collective-permute-done | bytes 65568 | tf_op jit(solution)/shard_map/cols/ppermute | solution.py:56
  26.8 0.1 collective-permute-start.6
  26.9 1.1 %collective-permute-done.16 = f32[128,128]{1,0:T(8,128)S(1)} collective-permute-done((f32[128,128]{1,0:T(8,128)S(1)}, f32[128,128]{1,0:T(8,128)S(1)}, u32[]{:S(2)}, u32[]{:S(2)}) %collective-permute-start.16) | collective-permute-done | bytes 65568 | tf_op jit(solution)/shard_map/diag/ppermute | solution.py:56
  28.0 1.4 %collective-permute-start.5 = (f32[128,128]{1,0:T(8,128)S(1)}, f32[128,128]{1,0:T(8,128)S(1)}, u32[]{:S(2)}, u32[]{:S(2)}) collective-permute-start(f32[128,128]{1,0:T(8,128)S(1)} %select_select_fusion.3), channel_id=1, source_target_pairs={{0,128},{1,129},{2,130},{3,131},{4,132},{5,133},{6,134},{7,135},{8... | collective-permute-start | bytes 196616 | tf_op jit(solution)/shard_map/cols/ppermute | solution.py:56
  29.4 2.5 %collective-permute-start.4 = (f32[128,128]{1,0:T(8,128)S(1)}, f32[128,128]{1,0:T(8,128)S(1)}, u32[]{:S(2)}, u32[]{:S(2)}) collective-permute-start(f32[128,128]{1,0:T(8,128)S(1)} %select_select_fusion.3), channel_id=1, source_target_pairs={{0,192},{1,193},{2,194},{3,195},{4,196},{5,197},{6,198},{7,199},{8... | collective-permute-start | bytes 196616 | tf_op jit(solution)/shard_map/cols/ppermute | solution.py:56
  31.9 2.4 %collective-permute-done.18 = f32[512,128]{1,0:T(8,128)S(1)} collective-permute-done((f32[512,128]{1,0:T(8,128)S(1)}, f32[512,128]{1,0:T(8,128)S(1)}, u32[]{:S(2)}, u32[]{:S(2)}) %collective-permute-start.18) | collective-permute-done | bytes 262176 | tf_op jit(solution)/shard_map/rows/ppermute | solution.py:56
  34.3 0.7 %collective-permute-start.25 = (f32[128,128]{1,0:T(8,128)S(1)}, f32[128,128]{1,0:T(8,128)S(1)}, u32[]{:S(2)}, u32[]{:S(2)}) collective-permute-start(f32[128,128]{1,0:T(8,128)S(1)} %select_select_fusion.own_ref), channel_id=1, source_target_pairs={{0,9},{1,8},{2,11},{3,10},{4,13},{5,12},{6,15},{7,14},{8,1},{9,0},... | collective-permute-start | bytes 196616 | tf_op jit(solution)/shard_map/diag/ppermute | solution.py:56
  35.0 1.9 %collective-permute-start.24 = (f32[128,128]{1,0:T(8,128)S(1)}, f32[128,128]{1,0:T(8,128)S(1)}, u32[]{:S(2)}, u32[]{:S(2)}) collective-permute-start(f32[128,128]{1,0:T(8,128)S(1)} %select_select_fusion.own_ref), channel_id=1, source_target_pairs={{0,8},{1,9},{2,10},{3,11},{4,12},{5,13},{6,14},{7,15},{8,0},{9,1},... | collective-permute-start | bytes 196616 | tf_op jit(solution)/shard_map/diag/ppermute | solution.py:56
  36.9 0.0 collective-permute-done.6
  36.9 1.3 %collective-permute-start.23 = (f32[128,128]{1,0:T(8,128)S(1)}, f32[128,128]{1,0:T(8,128)S(1)}, u32[]{:S(2)}, u32[]{:S(2)}) collective-permute-start(f32[128,128]{1,0:T(8,128)S(1)} %select_select_fusion.own_ref), channel_id=1, source_target_pairs={{0,1},{1,0},{2,3},{3,2},{4,5},{5,4},{6,7},{7,6},{8,9},{9,8},{10,11... | collective-permute-start | bytes 196616 | tf_op jit(solution)/shard_map/diag/ppermute | solution.py:56
  38.2 0.1 collective-permute-start.22
  38.3 4.8 %collective-permute-start.21 = (f32[512,128]{1,0:T(8,128)S(1)}, f32[512,128]{1,0:T(8,128)S(1)}, u32[]{:S(2)}, u32[]{:S(2)}) collective-permute-start(f32[512,128]{1,0:T(8,128)S(1)} %pad_maximum_fusion.mine_ref), channel_id=1, source_target_pairs={{0,48},{1,49},{2,50},{3,51},{4,52},{5,53},{6,54},{7,55},{8,56},{9,... | collective-permute-start | bytes 786440 | tf_op jit(solution)/shard_map/cols/ppermute | solution.py:56
  43.2 0.0 collective-permute-done.25.both_ref
  43.2 1.1 %collective-permute-start.20 = (f32[512,128]{1,0:T(8,128)S(1)}, f32[512,128]{1,0:T(8,128)S(1)}, u32[]{:S(2)}, u32[]{:S(2)}) collective-permute-start(f32[512,128]{1,0:T(8,128)S(1)} %pad_maximum_fusion.mine_ref), channel_id=1, source_target_pairs={{0,8},{1,9},{2,10},{3,11},{4,12},{5,13},{6,14},{7,15},{8,0},{9,1},... | collective-permute-start | bytes 786440 | tf_op jit(solution)/shard_map/cols/ppermute | solution.py:56
  44.3 1.1 %collective-permute-start.7 = (f32[512,128]{1,0:T(8,128)S(1)}, f32[512,128]{1,0:T(8,128)S(1)}, u32[]{:S(2)}, u32[]{:S(2)}) collective-permute-start(f32[512,128]{1,0:T(8,128)S(1)} %pad_maximum_fusion.mine_ref), channel_id=1, source_target_pairs={{0,32},{1,33},{2,34},{3,35},{4,36},{5,37},{6,38},{7,39},{8,40},{9,... | collective-permute-start | bytes 786440 | tf_op jit(solution)/shard_map/cols/ppermute | solution.py:56
  45.4 0.5 collective-permute-start.19
  45.9 8.3 %factorize.1 = (f32[256,256]{1,0:T(8,128)S(1)}, f32[256,256]{1,0:T(8,128)S(1)}) custom-call(s32[6]{0:T(128)S(1)} %stack.31.pos_ref, f32[128,128]{1,0:T(8,128)S(1)} %select_select_fusion.own_ref, f32[128,128]{1,0:T(8,128)S(1)} %collective-permute-done.23.across_ref, f32[128,128]{1,0:T(8,128)S(1)} %collective-permute-done.24.core_ref, ...), custom_call_target="tpu_custom_call" | custom-call | flops 4000000000 | bytes 800000 | tf_op jit(solution)/shard_map/diag/factorize/pallas_call | solution.py:175
  54.2 0.0 copy-start.1
  54.2 0.0 collective-permute-done.22.down_ref
  54.2 1.1 %collective-permute-start.26 = (f32[512,128]{1,0:T(8,128)S(1)}, f32[512,128]{1,0:T(8,128)S(1)}, u32[]{:S(2)}, u32[]{:S(2)}) collective-permute-start(f32[512,128]{1,0:T(8,128)S(1)} %collective-permute-done.21.up_ref), channel_id=1, source_target_pairs={{0,8},{1,9},{2,10},{3,11},{4,12},{5,13},{6,14},{7,15},{8,0},{9,1},... | collective-permute-start | bytes 786440 | tf_op jit(solution)/shard_map/cols/ppermute | solution.py:56
  55.3 0.0 collective-permute-start.27
  55.3 0.0 collective-permute-done.20.other_ref
  55.3 1.2 %solve_early.1 = (f32[512,256]{1,0:T(8,128)S(1)}, f32[256,512]{1,0:T(8,128)S(1)}) custom-call(s32[6]{0:T(128)S(1)} %stack.31.pos_ref, f32[512,128]{1,0:T(8,128)S(1)} %broadcast_select_fusion.1.near_ref, f32[512,128]{1,0:T(8,128)S(1)} %collective-permute-done.19.far_ref, f32[512,128]{1,0:T(8,128)S(1)} %pad_maximum_fusion.mine_ref, ...), custom_call_target="tpu_custom_call" | custom-call | flops 1000000000 | bytes 3000000 | tf_op jit(solution)/shard_map/cols/solve_early/pallas_call | solution.py:199
  56.5 0.8 %collective-permute-start.28 = (f32[512,128]{1,0:T(8,128)S(1)}, f32[512,128]{1,0:T(8,128)S(1)}, u32[]{:S(2)}, u32[]{:S(2)}) collective-permute-start(f32[512,128]{1,0:T(8,128)S(1)} %collective-permute-done.7.refs_4_), channel_id=1, source_target_pairs={{0,8},{1,9},{2,10},{3,11},{4,12},{5,13},{6,14},{7,15},{8,0},{9,1},... | collective-permute-start | bytes 786440 | tf_op jit(solution)/shard_map/cols/ppermute | solution.py:56
  57.3 1.2 %solve_sides.1 = (f32[256,512]{1,0:T(8,128)S(1)}, f32[256,512]{1,0:T(8,128)S(1)}) custom-call(s32[6]{0:T(128)S(1)} %stack.31.pos_ref, f32[512,128]{1,0:T(8,128)S(1)} %collective-permute-done.21.up_ref, f32[512,128]{1,0:T(8,128)S(1)} %collective-permute-done.26.up_other_ref, f32[512,128]{1,0:T(8,128)S(1)} %collective-permute-done.22.down_ref, ...), custom_call_target="tpu_custom_call" | custom-call | flops 1000000000 | bytes 3000000 | tf_op jit(solution)/shard_map/cols/solve_sides/pallas_call | solution.py:223
  58.5 6.1 %update.1 = f32[8192,128]{1,0:T(8,128)} custom-call(s32[6]{0:T(128)S(1)} %stack.31.pos_ref, f32[8192,128]{1,0:T(8,128)S(1)} %bitcast.12, f32[512,256]{1,0:T(8,128)S(1)} %get-tuple-element.35.refs_0_, f32[256,512]{1,0:T(8,128)S(1)} %get-tuple-element.36.refs_1_, f32[256,512]{1,0:T(8,128)S(1)} %get-tuple-element.39.refs_2_, ...), custom_call_target="tpu_custom_call" | custom-call | flops 3000000000 | bytes 12000000 | tf_op jit(solution)/shard_map/final/update/pallas_call | solution.py:293
  (28 shorter events, 0.2 us)
Async XLA Ops:
  0.1 2.2 %copy-start = (f32[4,1,128,16,1,128]{5,4,3,2,1,0:T(1,128)S(1)}, f32[4,1,128,16,1,128]{5,4,3,2,1,0:T(1,128)}, u32[]{:S(2)}) copy-start(f32[4,1,128,16,1,128]{5,4,3,2,1,0:T(1,128)} %param.1) | copy-start | bytes 12582916
  3.0 5.5 %collective-permute-start.10 = (f32[128,128]{1,0:T(8,128)S(1)}, f32[128,128]{1,0:T(8,128)S(1)}, u32[]{:S(2)}, u32[]{:S(2)}) collective-permute-start(f32[128,128]{1,0:T(8,128)S(1)} %slice.3), channel_id=1, source_target_pairs={{0,3},{1,2},{2,1},{3,0},{4,12},{5,13},{6,14},{7,15},{8,11},{9,10},... | collective-permute-start | bytes 196616 | tf_op jit(solution)/shard_map/diag/ppermute | solution.py:56
  6.4 3.1 %collective-permute-start.9 = (f32[128,128]{1,0:T(8,128)S(1)}, f32[128,128]{1,0:T(8,128)S(1)}, u32[]{:S(2)}, u32[]{:S(2)}) collective-permute-start(f32[128,128]{1,0:T(8,128)S(1)} %slice.3), channel_id=1, source_target_pairs={{0,4},{1,5},{2,10},{3,11},{4,0},{5,1},{6,14},{7,15},{8,12},{9,13},... | collective-permute-start | bytes 196616 | tf_op jit(solution)/shard_map/diag/ppermute | solution.py:56
  6.4 5.3 %collective-permute-start.8 = (f32[128,128]{1,0:T(8,128)S(1)}, f32[128,128]{1,0:T(8,128)S(1)}, u32[]{:S(2)}, u32[]{:S(2)}) collective-permute-start(f32[128,128]{1,0:T(8,128)S(1)} %slice.3), channel_id=1, source_target_pairs={{0,7},{1,6},{2,10},{3,11},{4,12},{5,13},{6,1},{7,0},{8,15},{9,14},... | collective-permute-start | bytes 196616 | tf_op jit(solution)/shard_map/diag/ppermute | solution.py:56
  11.8 4.0 %collective-permute-start.13 = (f32[128,128]{1,0:T(8,128)S(1)}, f32[128,128]{1,0:T(8,128)S(1)}, u32[]{:S(2)}, u32[]{:S(2)}) collective-permute-start(f32[128,128]{1,0:T(8,128)S(1)} %select_select_fusion.2), channel_id=1, source_target_pairs={{0,16},{1,17},{2,18},{3,19},{4,20},{5,21},{6,22},{7,23},{8,24},{9,... | collective-permute-start | bytes 196616 | tf_op jit(solution)/shard_map/diag/ppermute | solution.py:56
  11.9 7.9 %collective-permute-start.12 = (f32[128,128]{1,0:T(8,128)S(1)}, f32[128,128]{1,0:T(8,128)S(1)}, u32[]{:S(2)}, u32[]{:S(2)}) collective-permute-start(f32[128,128]{1,0:T(8,128)S(1)} %select_select_fusion.2), channel_id=1, source_target_pairs={{0,48},{1,49},{2,50},{3,51},{4,52},{5,53},{6,54},{7,55},{8,56},{9,... | collective-permute-start | bytes 196616 | tf_op jit(solution)/shard_map/diag/ppermute | solution.py:56
  12.0 7.8 %collective-permute-start.11 = (f32[128,128]{1,0:T(8,128)S(1)}, f32[128,128]{1,0:T(8,128)S(1)}, u32[]{:S(2)}, u32[]{:S(2)}) collective-permute-start(f32[128,128]{1,0:T(8,128)S(1)} %select_select_fusion.2), channel_id=1, source_target_pairs={{0,32},{1,33},{2,34},{3,35},{4,36},{5,37},{6,38},{7,39},{8,40},{9,... | collective-permute-start | bytes 196616 | tf_op jit(solution)/shard_map/diag/ppermute | solution.py:56
  12.1 9.7 %collective-permute-start.17 = (f32[512,128]{1,0:T(8,128)S(1)}, f32[512,128]{1,0:T(8,128)S(1)}, u32[]{:S(2)}, u32[]{:S(2)}) collective-permute-start(f32[512,128]{1,0:T(8,128)S(1)} %get-tuple-element.28), channel_id=1, source_target_pairs={{0,4},{1,5},{2,10},{3,11},{4,0},{5,1},{6,14},{7,15},{8,12},{9,13},... | collective-permute-start | bytes 786440 | tf_op jit(solution)/shard_map/rows/ppermute | solution.py:56
  12.2 9.7 %collective-permute-start = (f32[128,128]{1,0:T(8,128)S(1)}, f32[128,128]{1,0:T(8,128)S(1)}, u32[]{:S(2)}, u32[]{:S(2)}) collective-permute-start(f32[128,128]{1,0:T(8,128)S(1)} %get-tuple-element.24), channel_id=1, source_target_pairs={{0,48},{1,56},{2,16},{3,24},{4,12},{5,13},{6,14},{7,15},{8,49},{9,... | collective-permute-start | bytes 196616 | tf_op jit(solution)/shard_map/cols/ppermute | solution.py:56
  15.8 7.0 %collective-permute-start.1 = (f32[128,128]{1,0:T(8,128)S(1)}, f32[128,128]{1,0:T(8,128)S(1)}, u32[]{:S(2)}, u32[]{:S(2)}) collective-permute-start(f32[128,128]{1,0:T(8,128)S(1)} %get-tuple-element.25), channel_id=1, source_target_pairs={{0,32},{1,40},{2,10},{3,11},{4,0},{5,1},{6,14},{7,15},{8,33},{9,41... | collective-permute-start | bytes 196616 | tf_op jit(solution)/shard_map/cols/ppermute | solution.py:56
  19.8 7.0 %collective-permute-start.2 = (f32[128,128]{1,0:T(8,128)S(1)}, f32[128,128]{1,0:T(8,128)S(1)}, u32[]{:S(2)}, u32[]{:S(2)}) collective-permute-start(f32[128,128]{1,0:T(8,128)S(1)} %get-tuple-element.26), channel_id=1, source_target_pairs={{0,16},{1,24},{2,10},{3,11},{4,12},{5,13},{6,48},{7,56},{8,17},{9,... | collective-permute-start | bytes 196616 | tf_op jit(solution)/shard_map/cols/ppermute | solution.py:56
  19.8 7.0 %collective-permute-start.3 = (f32[128,128]{1,0:T(8,128)S(1)}, f32[128,128]{1,0:T(8,128)S(1)}, u32[]{:S(2)}, u32[]{:S(2)}) collective-permute-start(f32[128,128]{1,0:T(8,128)S(1)} %get-tuple-element.27), channel_id=1, source_target_pairs={{0,0},{1,8},{2,10},{3,11},{4,12},{5,13},{6,14},{7,15},{8,1},{9,9},... | collective-permute-start | bytes 196616 | tf_op jit(solution)/shard_map/cols/ppermute | solution.py:56
  21.7 6.3 %collective-permute-start.16 = (f32[128,128]{1,0:T(8,128)S(1)}, f32[128,128]{1,0:T(8,128)S(1)}, u32[]{:S(2)}, u32[]{:S(2)}) collective-permute-start(f32[128,128]{1,0:T(8,128)S(1)} %select_select_fusion.1), channel_id=1, source_target_pairs={{0,64},{1,65},{2,66},{3,67},{4,68},{5,69},{6,70},{7,71},{8,72},{9,... | collective-permute-start | bytes 196616 | tf_op jit(solution)/shard_map/diag/ppermute | solution.py:56
  21.9 7.5 %collective-permute-start.15 = (f32[128,128]{1,0:T(8,128)S(1)}, f32[128,128]{1,0:T(8,128)S(1)}, u32[]{:S(2)}, u32[]{:S(2)}) collective-permute-start(f32[128,128]{1,0:T(8,128)S(1)} %select_select_fusion.1), channel_id=1, source_target_pairs={{0,192},{1,193},{2,194},{3,195},{4,196},{5,197},{6,198},{7,199},{8... | collective-permute-start | bytes 196616 | tf_op jit(solution)/shard_map/diag/ppermute | solution.py:56
  22.8 9.1 %collective-permute-start.14 = (f32[128,128]{1,0:T(8,128)S(1)}, f32[128,128]{1,0:T(8,128)S(1)}, u32[]{:S(2)}, u32[]{:S(2)}) collective-permute-start(f32[128,128]{1,0:T(8,128)S(1)} %select_select_fusion.1), channel_id=1, source_target_pairs={{0,128},{1,129},{2,130},{3,131},{4,132},{5,133},{6,134},{7,135},{8... | collective-permute-start | bytes 196616 | tf_op jit(solution)/shard_map/diag/ppermute | solution.py:56
  26.8 7.5 %collective-permute-start.18 = (f32[512,128]{1,0:T(8,128)S(1)}, f32[512,128]{1,0:T(8,128)S(1)}, u32[]{:S(2)}, u32[]{:S(2)}) collective-permute-start(f32[512,128]{1,0:T(8,128)S(1)} %broadcast_select_fusion), channel_id=1, source_target_pairs={{0,3},{1,2},{2,1},{3,0},{4,7},{5,6},{6,5},{7,4},{8,11},{9,10},{10,... | collective-permute-start | bytes 786440 | tf_op jit(solution)/shard_map/rows/ppermute | solution.py:56
  26.8 10.1 %collective-permute-start.6 = (f32[128,128]{1,0:T(8,128)S(1)}, f32[128,128]{1,0:T(8,128)S(1)}, u32[]{:S(2)}, u32[]{:S(2)}) collective-permute-start(f32[128,128]{1,0:T(8,128)S(1)} %select_select_fusion.3), channel_id=1, source_target_pairs={{0,64},{1,65},{2,66},{3,67},{4,68},{5,69},{6,70},{7,71},{8,72},{9,... | collective-permute-start | bytes 196616 | tf_op jit(solution)/shard_map/cols/ppermute | solution.py:56
  28.0 10.2 %collective-permute-start.5 = (f32[128,128]{1,0:T(8,128)S(1)}, f32[128,128]{1,0:T(8,128)S(1)}, u32[]{:S(2)}, u32[]{:S(2)}) collective-permute-start(f32[128,128]{1,0:T(8,128)S(1)} %select_select_fusion.3), channel_id=1, source_target_pairs={{0,128},{1,129},{2,130},{3,131},{4,132},{5,133},{6,134},{7,135},{8... | collective-permute-start | bytes 196616 | tf_op jit(solution)/shard_map/cols/ppermute | solution.py:56
  29.4 8.8 %collective-permute-start.4 = (f32[128,128]{1,0:T(8,128)S(1)}, f32[128,128]{1,0:T(8,128)S(1)}, u32[]{:S(2)}, u32[]{:S(2)}) collective-permute-start(f32[128,128]{1,0:T(8,128)S(1)} %select_select_fusion.3), channel_id=1, source_target_pairs={{0,192},{1,193},{2,194},{3,195},{4,196},{5,197},{6,198},{7,199},{8... | collective-permute-start | bytes 196616 | tf_op jit(solution)/shard_map/cols/ppermute | solution.py:56
  34.3 8.9 %collective-permute-start.25 = (f32[128,128]{1,0:T(8,128)S(1)}, f32[128,128]{1,0:T(8,128)S(1)}, u32[]{:S(2)}, u32[]{:S(2)}) collective-permute-start(f32[128,128]{1,0:T(8,128)S(1)} %select_select_fusion.own_ref), channel_id=1, source_target_pairs={{0,9},{1,8},{2,11},{3,10},{4,13},{5,12},{6,15},{7,14},{8,1},{9,0},... | collective-permute-start | bytes 196616 | tf_op jit(solution)/shard_map/diag/ppermute | solution.py:56
  35.0 9.3 %collective-permute-start.24 = (f32[128,128]{1,0:T(8,128)S(1)}, f32[128,128]{1,0:T(8,128)S(1)}, u32[]{:S(2)}, u32[]{:S(2)}) collective-permute-start(f32[128,128]{1,0:T(8,128)S(1)} %select_select_fusion.own_ref), channel_id=1, source_target_pairs={{0,8},{1,9},{2,10},{3,11},{4,12},{5,13},{6,14},{7,15},{8,0},{9,1},... | collective-permute-start | bytes 196616 | tf_op jit(solution)/shard_map/diag/ppermute | solution.py:56
  36.9 8.5 %collective-permute-start.23 = (f32[128,128]{1,0:T(8,128)S(1)}, f32[128,128]{1,0:T(8,128)S(1)}, u32[]{:S(2)}, u32[]{:S(2)}) collective-permute-start(f32[128,128]{1,0:T(8,128)S(1)} %select_select_fusion.own_ref), channel_id=1, source_target_pairs={{0,1},{1,0},{2,3},{3,2},{4,5},{5,4},{6,7},{7,6},{8,9},{9,8},{10,11... | collective-permute-start | bytes 196616 | tf_op jit(solution)/shard_map/diag/ppermute | solution.py:56
  38.2 16.0 %collective-permute-start.22 = (f32[512,128]{1,0:T(8,128)S(1)}, f32[512,128]{1,0:T(8,128)S(1)}, u32[]{:S(2)}, u32[]{:S(2)}) collective-permute-start(f32[512,128]{1,0:T(8,128)S(1)} %pad_maximum_fusion.mine_ref), channel_id=1, source_target_pairs={{0,16},{1,17},{2,18},{3,19},{4,20},{5,21},{6,22},{7,23},{8,24},{9,... | collective-permute-start | bytes 786440 | tf_op jit(solution)/shard_map/cols/ppermute | solution.py:56
  38.3 15.9 %collective-permute-start.21 = (f32[512,128]{1,0:T(8,128)S(1)}, f32[512,128]{1,0:T(8,128)S(1)}, u32[]{:S(2)}, u32[]{:S(2)}) collective-permute-start(f32[512,128]{1,0:T(8,128)S(1)} %pad_maximum_fusion.mine_ref), channel_id=1, source_target_pairs={{0,48},{1,49},{2,50},{3,51},{4,52},{5,53},{6,54},{7,55},{8,56},{9,... | collective-permute-start | bytes 786440 | tf_op jit(solution)/shard_map/cols/ppermute | solution.py:56
  43.2 12.2 %collective-permute-start.20 = (f32[512,128]{1,0:T(8,128)S(1)}, f32[512,128]{1,0:T(8,128)S(1)}, u32[]{:S(2)}, u32[]{:S(2)}) collective-permute-start(f32[512,128]{1,0:T(8,128)S(1)} %pad_maximum_fusion.mine_ref), channel_id=1, source_target_pairs={{0,8},{1,9},{2,10},{3,11},{4,12},{5,13},{6,14},{7,15},{8,0},{9,1},... | collective-permute-start | bytes 786440 | tf_op jit(solution)/shard_map/cols/ppermute | solution.py:56
  44.3 12.2 %collective-permute-start.7 = (f32[512,128]{1,0:T(8,128)S(1)}, f32[512,128]{1,0:T(8,128)S(1)}, u32[]{:S(2)}, u32[]{:S(2)}) collective-permute-start(f32[512,128]{1,0:T(8,128)S(1)} %pad_maximum_fusion.mine_ref), channel_id=1, source_target_pairs={{0,32},{1,33},{2,34},{3,35},{4,36},{5,37},{6,38},{7,39},{8,40},{9,... | collective-permute-start | bytes 786440 | tf_op jit(solution)/shard_map/cols/ppermute | solution.py:56
  45.4 9.9 %collective-permute-start.19 = (f32[512,128]{1,0:T(8,128)S(1)}, f32[512,128]{1,0:T(8,128)S(1)}, u32[]{:S(2)}, u32[]{:S(2)}) collective-permute-start(f32[512,128]{1,0:T(8,128)S(1)} %broadcast_select_fusion.1.near_ref), channel_id=1, source_target_pairs={{0,1},{1,0},{2,3},{3,2},{4,5},{5,4},{6,7},{7,6},{8,9},{9,8},{10,11... | collective-permute-start | bytes 786440 | tf_op jit(solution)/shard_map/diag/ppermute | solution.py:56
  54.2 4.3 %copy-start.1 = (f32[4,1,128,16,1,128]{5,4,3,2,1,0:T(1,128)S(1)}, f32[4,1,128,16,1,128]{5,4,3,2,1,0:T(1,128)}, u32[]{:S(2)}) copy-start(f32[4,1,128,16,1,128]{5,4,3,2,1,0:T(1,128)} %param.1) | copy-start | bytes 12582916
  54.2 3.1 %collective-permute-start.26 = (f32[512,128]{1,0:T(8,128)S(1)}, f32[512,128]{1,0:T(8,128)S(1)}, u32[]{:S(2)}, u32[]{:S(2)}) collective-permute-start(f32[512,128]{1,0:T(8,128)S(1)} %collective-permute-done.21.up_ref), channel_id=1, source_target_pairs={{0,8},{1,9},{2,10},{3,11},{4,12},{5,13},{6,14},{7,15},{8,0},{9,1},... | collective-permute-start | bytes 786440 | tf_op jit(solution)/shard_map/cols/ppermute | solution.py:56
  55.3 2.0 %collective-permute-start.27 = (f32[512,128]{1,0:T(8,128)S(1)}, f32[512,128]{1,0:T(8,128)S(1)}, u32[]{:S(2)}, u32[]{:S(2)}) collective-permute-start(f32[512,128]{1,0:T(8,128)S(1)} %collective-permute-done.22.down_ref), channel_id=1, source_target_pairs={{0,8},{1,9},{2,10},{3,11},{4,12},{5,13},{6,14},{7,15},{8,0},{9,1},... | collective-permute-start | bytes 786440 | tf_op jit(solution)/shard_map/cols/ppermute | solution.py:56
  56.5 2.0 %collective-permute-start.28 = (f32[512,128]{1,0:T(8,128)S(1)}, f32[512,128]{1,0:T(8,128)S(1)}, u32[]{:S(2)}, u32[]{:S(2)}) collective-permute-start(f32[512,128]{1,0:T(8,128)S(1)} %collective-permute-done.7.refs_4_), channel_id=1, source_target_pairs={{0,8},{1,9},{2,10},{3,11},{4,12},{5,13},{6,14},{7,15},{8,0},{9,1},... | collective-permute-start | bytes 786440 | tf_op jit(solution)/shard_map/cols/ppermute | solution.py:56

commit v4 on v3

--- a/solution.py
+++ b/solution.py
@@ -349,10 +349,10 @@
         ]
         for which, targets in zip(arrivals, stages):
             diag = spread(which, diag, [diag] * 3, targets)
-        diag, near = lax.optimization_barrier((diag, near))
         across = send(diag, lambda zh, y, core, zl, x: (zh, y, core, zl, x ^ 1))
         both = send(diag, lambda zh, y, core, zl, x: (zh, y, 1 - core, zl, x ^ 1))
-        cored = send(diag, lambda zh, y, core, zl, x: (zh, y, 1 - core, zl, x))
+        tied, near = lax.optimization_barrier((diag, near))
+        cored = send(tied, lambda zh, y, core, zl, x: (zh, y, 1 - core, zl, x))
         far = send(near, lambda zh, y, core, zl, x: (zh, y, core, zl, x ^ 1))
         upper, inverse = factorize(pos, diag, across, cored, both)
 

time: 64.8 us -> 64.8 us (level)
  starting transfers between devices: 35.2 us -> 37.6 us
  waiting for transfers between devices: 9.35 us -> 6.97 us
    ppermute x29, starting transfers between devices: 35.2 us -> 37.6 us  [send(): return lax.ppermute(value, AXES, closed(pairs_of(target)))]
    ppermute x29, waiting for transfers between devices: 9.35 us -> 6.97 us  [send(): return lax.ppermute(value, AXES, closed(pairs_of(target)))]
  transfers between devices with their start and end apart: 29 -> 29, of which waited for: 5 -> 4; matrix products, arithmetic and copies ran while one was open for 0% -> 0% of each run, Pallas kernels for 16% -> 16%
where the time goes in v4:
time: 64.8 us; the launch traced here: 64.7 us
  starting transfers between devices  37.6 us (58%)
  Pallas kernels  17.5 us (27%)
  waiting for transfers between devices  6.97 us (11%)
  local copies, waits for them, and re-layouts  2.28 us (4%)
    ppermute x29, starting transfers between devices, send(): return lax.ppermute(value, AXES, closed(pairs_of(target)))  37.6 us
    pallas_call x1, Pallas kernels, factorize(): pl.pallas_call(functools.partial(factor_kernel, 32), out_shape=[square, s...  8.27 us
    ppermute x29, waiting for transfers between devices, send(): return lax.ppermute(value, AXES, closed(pairs_of(target)))  6.97 us
    pallas_call x1, Pallas kernels, update(): pl.pallas_call(functools.partial(update_kernel, rows), grid=(512 // rows,...  6.15 us
    unnamed x4, local copies, waits for them, and re-layouts  2.2 us
  transfers between devices with their start and end apart: 29, of which 4 were waited for; matrix products, arithmetic and copies ran while one was open for 0% of the time, Pallas kernels for 16%

profile of v4, /device:TPU:1, one launch (start us, length us, event | category | flops | bytes accessed | tf_op | source)
XLA Modules:
  0.0 64.7 jit_solution(15207370173883540827)
XLA Ops:
  0.0 0.1 stack.31.pos_ref
  0.1 2.2 %copy-done = f32[4,1,128,16,1,128]{5,4,3,2,1,0:T(1,128)S(1)} copy-done((f32[4,1,128,16,1,128]{5,4,3,2,1,0:T(1,128)S(1)}, f32[4,1,128,16,1,128]{5,4,3,2,1,0:T(1,128)}, u32[]{:S(2)}) %copy-start) | copy-done | bytes 4194328
  2.3 0.7 %prepare.1 = (f32[512,128]{1,0:T(8,128)S(1)}, f32[128,128]{1,0:T(8,128)S(1)}, f32[128,128]{1,0:T(8,128)S(1)}, f32[128,128]{1,0:T(8,128)S(1)}, f32[128,128]{1,0:T(8,128)S(1)}) custom-call(s32[6]{0:T(128)S(1)} %stack.31.pos_ref, f32[512,16,128]{2,1,0:T(8,128)S(1)} %bitcast.11), custom_call_target="tpu_custom_call" | custom-call | tf_op jit(solution)/shard_map/prepare/pallas_call | solution.py:102
  3.0 3.4 %collective-permute-start.10 = (f32[128,128]{1,0:T(8,128)S(1)}, f32[128,128]{1,0:T(8,128)S(1)}, u32[]{:S(2)}, u32[]{:S(2)}) collective-permute-start(f32[128,128]{1,0:T(8,128)S(1)} %slice.3), channel_id=1, source_target_pairs={{0,3},{1,2},{2,1},{3,0},{4,12},{5,13},{6,14},{7,15},{8,11},{9,10},... | collective-permute-start | bytes 196616 | tf_op jit(solution)/shard_map/diag/ppermute | solution.py:56
  6.4 0.0 collective-permute-start.9
  6.4 2.1 %collective-permute-start.8 = (f32[128,128]{1,0:T(8,128)S(1)}, f32[128,128]{1,0:T(8,128)S(1)}, u32[]{:S(2)}, u32[]{:S(2)}) collective-permute-start(f32[128,128]{1,0:T(8,128)S(1)} %slice.3), channel_id=1, source_target_pairs={{0,7},{1,6},{2,10},{3,11},{4,12},{5,13},{6,1},{7,0},{8,15},{9,14},... | collective-permute-start | bytes 196616 | tf_op jit(solution)/shard_map/diag/ppermute | solution.py:56
  8.5 0.0 collective-permute-done.10
  8.5 1.0 %collective-permute-done.9 = f32[128,128]{1,0:T(8,128)S(1)} collective-permute-done((f32[128,128]{1,0:T(8,128)S(1)}, f32[128,128]{1,0:T(8,128)S(1)}, u32[]{:S(2)}, u32[]{:S(2)}) %collective-permute-start.9) | collective-permute-done | bytes 65568 | tf_op jit(solution)/shard_map/diag/ppermute | solution.py:56
  9.5 2.2 %collective-permute-done.8 = f32[128,128]{1,0:T(8,128)S(1)} collective-permute-done((f32[128,128]{1,0:T(8,128)S(1)}, f32[128,128]{1,0:T(8,128)S(1)}, u32[]{:S(2)}, u32[]{:S(2)}) %collective-permute-start.8) | collective-permute-done | bytes 65568 | tf_op jit(solution)/shard_map/diag/ppermute | solution.py:56
  11.8 0.1 collective-permute-start.13
  11.9 0.1 collective-permute-start.12
  12.0 0.1 collective-permute-start.11
  12.1 0.1 collective-permute-start.17
  12.2 3.6 %collective-permute-start = (f32[128,128]{1,0:T(8,128)S(1)}, f32[128,128]{1,0:T(8,128)S(1)}, u32[]{:S(2)}, u32[]{:S(2)}) collective-permute-start(f32[128,128]{1,0:T(8,128)S(1)} %get-tuple-element.24), channel_id=1, source_target_pairs={{0,48},{1,56},{2,16},{3,24},{4,12},{5,13},{6,14},{7,15},{8,49},{9,... | collective-permute-start | bytes 196616 | tf_op jit(solution)/shard_map/cols/ppermute | solution.py:56
  15.8 0.0 collective-permute-done.13
  15.8 4.0 %collective-permute-start.1 = (f32[128,128]{1,0:T(8,128)S(1)}, f32[128,128]{1,0:T(8,128)S(1)}, u32[]{:S(2)}, u32[]{:S(2)}) collective-permute-start(f32[128,128]{1,0:T(8,128)S(1)} %get-tuple-element.25), channel_id=1, source_target_pairs={{0,32},{1,40},{2,10},{3,11},{4,0},{5,1},{6,14},{7,15},{8,33},{9,41... | collective-permute-start | bytes 196616 | tf_op jit(solution)/shard_map/cols/ppermute | solution.py:56
  19.7 0.0 collective-permute-done.12
  19.8 1.9 %collective-permute-start.3 = (f32[128,128]{1,0:T(8,128)S(1)}, f32[128,128]{1,0:T(8,128)S(1)}, u32[]{:S(2)}, u32[]{:S(2)}) collective-permute-start(f32[128,128]{1,0:T(8,128)S(1)} %get-tuple-element.27), channel_id=1, source_target_pairs={{0,0},{1,8},{2,10},{3,11},{4,12},{5,13},{6,14},{7,15},{8,1},{9,9},... | collective-permute-start | bytes 196616 | tf_op jit(solution)/shard_map/cols/ppermute | solution.py:56
  21.7 0.1 collective-permute-start.16
  21.9 0.9 %collective-permute-start.15 = (f32[128,128]{1,0:T(8,128)S(1)}, f32[128,128]{1,0:T(8,128)S(1)}, u32[]{:S(2)}, u32[]{:S(2)}) collective-permute-start(f32[128,128]{1,0:T(8,128)S(1)} %select_select_fusion.1), channel_id=1, source_target_pairs={{0,192},{1,193},{2,194},{3,195},{4,196},{5,197},{6,198},{7,199},{8... | collective-permute-start | bytes 196616 | tf_op jit(solution)/shard_map/diag/ppermute | solution.py:56
  22.8 0.0 collective-permute-done.1
  22.8 1.4 %collective-permute-start.14 = (f32[128,128]{1,0:T(8,128)S(1)}, f32[128,128]{1,0:T(8,128)S(1)}, u32[]{:S(2)}, u32[]{:S(2)}) collective-permute-start(f32[128,128]{1,0:T(8,128)S(1)} %select_select_fusion.1), channel_id=1, source_target_pairs={{0,128},{1,129},{2,130},{3,131},{4,132},{5,133},{6,134},{7,135},{8... | collective-permute-start | bytes 196616 | tf_op jit(solution)/shard_map/diag/ppermute | solution.py:56
  24.2 2.6 %collective-permute-done.2 = f32[128,128]{1,0:T(8,128)S(1)} collective-permute-done((f32[128,128]{1,0:T(8,128)S(1)}, f32[128,128]{1,0:T(8,128)S(1)}, u32[]{:S(2)}, u32[]{:S(2)}) %collective-permute-start.2) | collective-permute-done | bytes 65568 | tf_op jit(solution)/shard_map/cols/ppermute | solution.py:56
  26.8 0.1 collective-permute-start.6
  26.9 1.1 %collective-permute-done.16 = f32[128,128]{1,0:T(8,128)S(1)} collective-permute-done((f32[128,128]{1,0:T(8,128)S(1)}, f32[128,128]{1,0:T(8,128)S(1)}, u32[]{:S(2)}, u32[]{:S(2)}) %collective-permute-start.16) | collective-permute-done | bytes 65568 | tf_op jit(solution)/shard_map/diag/ppermute | solution.py:56
  28.0 1.4 %collective-permute-start.5 = (f32[128,128]{1,0:T(8,128)S(1)}, f32[128,128]{1,0:T(8,128)S(1)}, u32[]{:S(2)}, u32[]{:S(2)}) collective-permute-start(f32[128,128]{1,0:T(8,128)S(1)} %select_select_fusion.3), channel_id=1, source_target_pairs={{0,128},{1,129},{2,130},{3,131},{4,132},{5,133},{6,134},{7,135},{8... | collective-permute-start | bytes 196616 | tf_op jit(solution)/shard_map/cols/ppermute | solution.py:56
  29.4 2.5 %collective-permute-start.4 = (f32[128,128]{1,0:T(8,128)S(1)}, f32[128,128]{1,0:T(8,128)S(1)}, u32[]{:S(2)}, u32[]{:S(2)}) collective-permute-start(f32[128,128]{1,0:T(8,128)S(1)} %select_select_fusion.3), channel_id=1, source_target_pairs={{0,192},{1,193},{2,194},{3,195},{4,196},{5,197},{6,198},{7,199},{8... | collective-permute-start | bytes 196616 | tf_op jit(solution)/shard_map/cols/ppermute | solution.py:56
  31.9 3.0 %collective-permute-start.25 = (f32[128,128]{1,0:T(8,128)S(1)}, f32[128,128]{1,0:T(8,128)S(1)}, u32[]{:S(2)}, u32[]{:S(2)}) collective-permute-start(f32[128,128]{1,0:T(8,128)S(1)} %select_select_fusion.own_ref), channel_id=1, source_target_pairs={{0,9},{1,8},{2,11},{3,10},{4,13},{5,12},{6,15},{7,14},{8,1},{9,0},... | collective-permute-start | bytes 196616 | tf_op jit(solution)/shard_map/diag/ppermute | solution.py:56
  34.9 0.3 collective-permute-start.23
  35.3 0.0 collective-permute-done.6
  35.3 2.5 %collective-permute-start.24 = (f32[128,128]{1,0:T(8,128)S(1)}, f32[128,128]{1,0:T(8,128)S(1)}, u32[]{:S(2)}, u32[]{:S(2)}) collective-permute-start(f32[128,128]{1,0:T(8,128)S(1)} %select_select_fusion.own_ref), channel_id=1, source_target_pairs={{0,8},{1,9},{2,10},{3,11},{4,12},{5,13},{6,14},{7,15},{8,0},{9,1},... | collective-permute-start | bytes 196616 | tf_op jit(solution)/shard_map/diag/ppermute | solution.py:56
  37.7 0.0 collective-permute-done.4
  37.7 0.8 %collective-permute-start.22 = (f32[512,128]{1,0:T(8,128)S(1)}, f32[512,128]{1,0:T(8,128)S(1)}, u32[]{:S(2)}, u32[]{:S(2)}) collective-permute-start(f32[512,128]{1,0:T(8,128)S(1)} %pad_maximum_fusion.mine_ref), channel_id=1, source_target_pairs={{0,16},{1,17},{2,18},{3,19},{4,20},{5,21},{6,22},{7,23},{8,24},{9,... | collective-permute-start | bytes 786440 | tf_op jit(solution)/shard_map/cols/ppermute | solution.py:56
  38.5 4.6 %collective-permute-start.21 = (f32[512,128]{1,0:T(8,128)S(1)}, f32[512,128]{1,0:T(8,128)S(1)}, u32[]{:S(2)}, u32[]{:S(2)}) collective-permute-start(f32[512,128]{1,0:T(8,128)S(1)} %pad_maximum_fusion.mine_ref), channel_id=1, source_target_pairs={{0,48},{1,49},{2,50},{3,51},{4,52},{5,53},{6,54},{7,55},{8,56},{9,... | collective-permute-start | bytes 786440 | tf_op jit(solution)/shard_map/cols/ppermute | solution.py:56
  43.2 1.1 %collective-permute-start.20 = (f32[512,128]{1,0:T(8,128)S(1)}, f32[512,128]{1,0:T(8,128)S(1)}, u32[]{:S(2)}, u32[]{:S(2)}) collective-permute-start(f32[512,128]{1,0:T(8,128)S(1)} %pad_maximum_fusion.mine_ref), channel_id=1, source_target_pairs={{0,8},{1,9},{2,10},{3,11},{4,12},{5,13},{6,14},{7,15},{8,0},{9,1},... | collective-permute-start | bytes 786440 | tf_op jit(solution)/shard_map/cols/ppermute | solution.py:56
  44.3 1.1 %collective-permute-start.7 = (f32[512,128]{1,0:T(8,128)S(1)}, f32[512,128]{1,0:T(8,128)S(1)}, u32[]{:S(2)}, u32[]{:S(2)}) collective-permute-start(f32[512,128]{1,0:T(8,128)S(1)} %pad_maximum_fusion.mine_ref), channel_id=1, source_target_pairs={{0,32},{1,33},{2,34},{3,35},{4,36},{5,37},{6,38},{7,39},{8,40},{9,... | collective-permute-start | bytes 786440 | tf_op jit(solution)/shard_map/cols/ppermute | solution.py:56
  45.4 0.0 collective-permute-done.24.core_ref
  45.4 0.0 collective-permute-start.19
  45.4 8.3 %factorize.1 = (f32[256,256]{1,0:T(8,128)S(1)}, f32[256,256]{1,0:T(8,128)S(1)}) custom-call(s32[6]{0:T(128)S(1)} %stack.31.pos_ref, f32[128,128]{1,0:T(8,128)S(1)} %select_select_fusion.own_ref, f32[128,128]{1,0:T(8,128)S(1)} %collective-permute-done.23.across_ref, f32[128,128]{1,0:T(8,128)S(1)} %collective-permute-done.24.core_ref, ...), custom_call_target="tpu_custom_call" | custom-call | flops 4000000000 | bytes 800000 | tf_op jit(solution)/shard_map/diag/factorize/pallas_call | solution.py:175
  53.7 0.0 copy-start.1
  53.7 0.0 collective-permute-done.22.down_ref
  53.7 0.0 collective-permute-done.21.up_ref
  53.7 1.6 %collective-permute-start.26 = (f32[512,128]{1,0:T(8,128)S(1)}, f32[512,128]{1,0:T(8,128)S(1)}, u32[]{:S(2)}, u32[]{:S(2)}) collective-permute-start(f32[512,128]{1,0:T(8,128)S(1)} %collective-permute-done.21.up_ref), channel_id=1, source_target_pairs={{0,8},{1,9},{2,10},{3,11},{4,12},{5,13},{6,14},{7,15},{8,0},{9,1},... | collective-permute-start | bytes 786440 | tf_op jit(solution)/shard_map/cols/ppermute | solution.py:56
  55.3 0.0 collective-permute-start.27
  55.3 1.2 %solve_early.1 = (f32[512,256]{1,0:T(8,128)S(1)}, f32[256,512]{1,0:T(8,128)S(1)}) custom-call(s32[6]{0:T(128)S(1)} %stack.31.pos_ref, f32[512,128]{1,0:T(8,128)S(1)} %broadcast_select_fusion.1.near_ref, f32[512,128]{1,0:T(8,128)S(1)} %collective-permute-done.19.far_ref, f32[512,128]{1,0:T(8,128)S(1)} %pad_maximum_fusion.mine_ref, ...), custom_call_target="tpu_custom_call" | custom-call | flops 1000000000 | bytes 3000000 | tf_op jit(solution)/shard_map/cols/solve_early/pallas_call | solution.py:199
  56.5 0.8 %collective-permute-start.28 = (f32[512,128]{1,0:T(8,128)S(1)}, f32[512,128]{1,0:T(8,128)S(1)}, u32[]{:S(2)}, u32[]{:S(2)}) collective-permute-start(f32[512,128]{1,0:T(8,128)S(1)} %collective-permute-done.7.refs_4_), channel_id=1, source_target_pairs={{0,8},{1,9},{2,10},{3,11},{4,12},{5,13},{6,14},{7,15},{8,0},{9,1},... | collective-permute-start | bytes 786440 | tf_op jit(solution)/shard_map/cols/ppermute | solution.py:56
  57.3 1.2 %solve_sides.1 = (f32[256,512]{1,0:T(8,128)S(1)}, f32[256,512]{1,0:T(8,128)S(1)}) custom-call(s32[6]{0:T(128)S(1)} %stack.31.pos_ref, f32[512,128]{1,0:T(8,128)S(1)} %collective-permute-done.21.up_ref, f32[512,128]{1,0:T(8,128)S(1)} %collective-permute-done.26.up_other_ref, f32[512,128]{1,0:T(8,128)S(1)} %collective-permute-done.22.down_ref, ...), custom_call_target="tpu_custom_call" | custom-call | flops 1000000000 | bytes 3000000 | tf_op jit(solution)/shard_map/cols/solve_sides/pallas_call | solution.py:223
  58.5 6.1 %update.1 = f32[8192,128]{1,0:T(8,128)} custom-call(s32[6]{0:T(128)S(1)} %stack.31.pos_ref, f32[8192,128]{1,0:T(8,128)S(1)} %bitcast.12, f32[512,256]{1,0:T(8,128)S(1)} %get-tuple-element.35.refs_0_, f32[256,512]{1,0:T(8,128)S(1)} %get-tuple-element.36.refs_1_, f32[256,512]{1,0:T(8,128)S(1)} %get-tuple-element.39.refs_2_, ...), custom_call_target="tpu_custom_call" | custom-call | flops 3000000000 | bytes 12000000 | tf_op jit(solution)/shard_map/final/update/pallas_call | solution.py:293
  (28 shorter events, 0.2 us)
Async XLA Ops:
  0.1 2.2 %copy-start = (f32[4,1,128,16,1,128]{5,4,3,2,1,0:T(1,128)S(1)}, f32[4,1,128,16,1,128]{5,4,3,2,1,0:T(1,128)}, u32[]{:S(2)}) copy-start(f32[4,1,128,16,1,128]{5,4,3,2,1,0:T(1,128)} %param.1) | copy-start | bytes 12582916
  3.0 5.5 %collective-permute-start.10 = (f32[128,128]{1,0:T(8,128)S(1)}, f32[128,128]{1,0:T(8,128)S(1)}, u32[]{:S(2)}, u32[]{:S(2)}) collective-permute-start(f32[128,128]{1,0:T(8,128)S(1)} %slice.3), channel_id=1, source_target_pairs={{0,3},{1,2},{2,1},{3,0},{4,12},{5,13},{6,14},{7,15},{8,11},{9,10},... | collective-permute-start | bytes 196616 | tf_op jit(solution)/shard_map/diag/ppermute | solution.py:56
  6.4 3.1 %collective-permute-start.9 = (f32[128,128]{1,0:T(8,128)S(1)}, f32[128,128]{1,0:T(8,128)S(1)}, u32[]{:S(2)}, u32[]{:S(2)}) collective-permute-start(f32[128,128]{1,0:T(8,128)S(1)} %slice.3), channel_id=1, source_target_pairs={{0,4},{1,5},{2,10},{3,11},{4,0},{5,1},{6,14},{7,15},{8,12},{9,13},... | collective-permute-start | bytes 196616 | tf_op jit(solution)/shard_map/diag/ppermute | solution.py:56
  6.4 5.3 %collective-permute-start.8 = (f32[128,128]{1,0:T(8,128)S(1)}, f32[128,128]{1,0:T(8,128)S(1)}, u32[]{:S(2)}, u32[]{:S(2)}) collective-permute-start(f32[128,128]{1,0:T(8,128)S(1)} %slice.3), channel_id=1, source_target_pairs={{0,7},{1,6},{2,10},{3,11},{4,12},{5,13},{6,1},{7,0},{8,15},{9,14},... | collective-permute-start | bytes 196616 | tf_op jit(solution)/shard_map/diag/ppermute | solution.py:56
  11.8 4.0 %collective-permute-start.13 = (f32[128,128]{1,0:T(8,128)S(1)}, f32[128,128]{1,0:T(8,128)S(1)}, u32[]{:S(2)}, u32[]{:S(2)}) collective-permute-start(f32[128,128]{1,0:T(8,128)S(1)} %select_select_fusion.2), channel_id=1, source_target_pairs={{0,16},{1,17},{2,18},{3,19},{4,20},{5,21},{6,22},{7,23},{8,24},{9,... | collective-permute-start | bytes 196616 | tf_op jit(solution)/shard_map/diag/ppermute | solution.py:56
  11.9 7.9 %collective-permute-start.12 = (f32[128,128]{1,0:T(8,128)S(1)}, f32[128,128]{1,0:T(8,128)S(1)}, u32[]{:S(2)}, u32[]{:S(2)}) collective-permute-start(f32[128,128]{1,0:T(8,128)S(1)} %select_select_fusion.2), channel_id=1, source_target_pairs={{0,48},{1,49},{2,50},{3,51},{4,52},{5,53},{6,54},{7,55},{8,56},{9,... | collective-permute-start | bytes 196616 | tf_op jit(solution)/shard_map/diag/ppermute | solution.py:56
  12.0 7.8 %collective-permute-start.11 = (f32[128,128]{1,0:T(8,128)S(1)}, f32[128,128]{1,0:T(8,128)S(1)}, u32[]{:S(2)}, u32[]{:S(2)}) collective-permute-start(f32[128,128]{1,0:T(8,128)S(1)} %select_select_fusion.2), channel_id=1, source_target_pairs={{0,32},{1,33},{2,34},{3,35},{4,36},{5,37},{6,38},{7,39},{8,40},{9,... | collective-permute-start | bytes 196616 | tf_op jit(solution)/shard_map/diag/ppermute | solution.py:56
  12.1 9.7 %collective-permute-start.17 = (f32[512,128]{1,0:T(8,128)S(1)}, f32[512,128]{1,0:T(8,128)S(1)}, u32[]{:S(2)}, u32[]{:S(2)}) collective-permute-start(f32[512,128]{1,0:T(8,128)S(1)} %get-tuple-element.28), channel_id=1, source_target_pairs={{0,4},{1,5},{2,10},{3,11},{4,0},{5,1},{6,14},{7,15},{8,12},{9,13},... | collective-permute-start | bytes 786440 | tf_op jit(solution)/shard_map/rows/ppermute | solution.py:56
  12.2 9.7 %collective-permute-start = (f32[128,128]{1,0:T(8,128)S(1)}, f32[128,128]{1,0:T(8,128)S(1)}, u32[]{:S(2)}, u32[]{:S(2)}) collective-permute-start(f32[128,128]{1,0:T(8,128)S(1)} %get-tuple-element.24), channel_id=1, source_target_pairs={{0,48},{1,56},{2,16},{3,24},{4,12},{5,13},{6,14},{7,15},{8,49},{9,... | collective-permute-start | bytes 196616 | tf_op jit(solution)/shard_map/cols/ppermute | solution.py:56
  15.8 7.0 %collective-permute-start.1 = (f32[128,128]{1,0:T(8,128)S(1)}, f32[128,128]{1,0:T(8,128)S(1)}, u32[]{:S(2)}, u32[]{:S(2)}) collective-permute-start(f32[128,128]{1,0:T(8,128)S(1)} %get-tuple-element.25), channel_id=1, source_target_pairs={{0,32},{1,40},{2,10},{3,11},{4,0},{5,1},{6,14},{7,15},{8,33},{9,41... | collective-permute-start | bytes 196616 | tf_op jit(solution)/shard_map/cols/ppermute | solution.py:56
  19.8 7.0 %collective-permute-start.2 = (f32[128,128]{1,0:T(8,128)S(1)}, f32[128,128]{1,0:T(8,128)S(1)}, u32[]{:S(2)}, u32[]{:S(2)}) collective-permute-start(f32[128,128]{1,0:T(8,128)S(1)} %get-tuple-element.26), channel_id=1, source_target_pairs={{0,16},{1,24},{2,10},{3,11},{4,12},{5,13},{6,48},{7,56},{8,17},{9,... | collective-permute-start | bytes 196616 | tf_op jit(solution)/shard_map/cols/ppermute | solution.py:56
  19.8 7.0 %collective-permute-start.3 = (f32[128,128]{1,0:T(8,128)S(1)}, f32[128,128]{1,0:T(8,128)S(1)}, u32[]{:S(2)}, u32[]{:S(2)}) collective-permute-start(f32[128,128]{1,0:T(8,128)S(1)} %get-tuple-element.27), channel_id=1, source_target_pairs={{0,0},{1,8},{2,10},{3,11},{4,12},{5,13},{6,14},{7,15},{8,1},{9,9},... | collective-permute-start | bytes 196616 | tf_op jit(solution)/shard_map/cols/ppermute | solution.py:56
  21.7 6.3 %collective-permute-start.16 = (f32[128,128]{1,0:T(8,128)S(1)}, f32[128,128]{1,0:T(8,128)S(1)}, u32[]{:S(2)}, u32[]{:S(2)}) collective-permute-start(f32[128,128]{1,0:T(8,128)S(1)} %select_select_fusion.1), channel_id=1, source_target_pairs={{0,64},{1,65},{2,66},{3,67},{4,68},{5,69},{6,70},{7,71},{8,72},{9,... | collective-permute-start | bytes 196616 | tf_op jit(solution)/shard_map/diag/ppermute | solution.py:56
  21.9 7.5 %collective-permute-start.15 = (f32[128,128]{1,0:T(8,128)S(1)}, f32[128,128]{1,0:T(8,128)S(1)}, u32[]{:S(2)}, u32[]{:S(2)}) collective-permute-start(f32[128,128]{1,0:T(8,128)S(1)} %select_select_fusion.1), channel_id=1, source_target_pairs={{0,192},{1,193},{2,194},{3,195},{4,196},{5,197},{6,198},{7,199},{8... | collective-permute-start | bytes 196616 | tf_op jit(solution)/shard_map/diag/ppermute | solution.py:56
  22.8 9.1 %collective-permute-start.14 = (f32[128,128]{1,0:T(8,128)S(1)}, f32[128,128]{1,0:T(8,128)S(1)}, u32[]{:S(2)}, u32[]{:S(2)}) collective-permute-start(f32[128,128]{1,0:T(8,128)S(1)} %select_select_fusion.1), channel_id=1, source_target_pairs={{0,128},{1,129},{2,130},{3,131},{4,132},{5,133},{6,134},{7,135},{8... | collective-permute-start | bytes 196616 | tf_op jit(solution)/shard_map/diag/ppermute | solution.py:56
  26.8 8.2 %collective-permute-start.18 = (f32[512,128]{1,0:T(8,128)S(1)}, f32[512,128]{1,0:T(8,128)S(1)}, u32[]{:S(2)}, u32[]{:S(2)}) collective-permute-start(f32[512,128]{1,0:T(8,128)S(1)} %broadcast_select_fusion), channel_id=1, source_target_pairs={{0,3},{1,2},{2,1},{3,0},{4,7},{5,6},{6,5},{7,4},{8,11},{9,10},{10,... | collective-permute-start | bytes 786440 | tf_op jit(solution)/shard_map/rows/ppermute | solution.py:56
  26.8 8.4 %collective-permute-start.6 = (f32[128,128]{1,0:T(8,128)S(1)}, f32[128,128]{1,0:T(8,128)S(1)}, u32[]{:S(2)}, u32[]{:S(2)}) collective-permute-start(f32[128,128]{1,0:T(8,128)S(1)} %select_select_fusion.3), channel_id=1, source_target_pairs={{0,64},{1,65},{2,66},{3,67},{4,68},{5,69},{6,70},{7,71},{8,72},{9,... | collective-permute-start | bytes 196616 | tf_op jit(solution)/shard_map/cols/ppermute | solution.py:56
  28.0 9.7 %collective-permute-start.5 = (f32[128,128]{1,0:T(8,128)S(1)}, f32[128,128]{1,0:T(8,128)S(1)}, u32[]{:S(2)}, u32[]{:S(2)}) collective-permute-start(f32[128,128]{1,0:T(8,128)S(1)} %select_select_fusion.3), channel_id=1, source_target_pairs={{0,128},{1,129},{2,130},{3,131},{4,132},{5,133},{6,134},{7,135},{8... | collective-permute-start | bytes 196616 | tf_op jit(solution)/shard_map/cols/ppermute | solution.py:56
  29.4 8.3 %collective-permute-start.4 = (f32[128,128]{1,0:T(8,128)S(1)}, f32[128,128]{1,0:T(8,128)S(1)}, u32[]{:S(2)}, u32[]{:S(2)}) collective-permute-start(f32[128,128]{1,0:T(8,128)S(1)} %select_select_fusion.3), channel_id=1, source_target_pairs={{0,192},{1,193},{2,194},{3,195},{4,196},{5,197},{6,198},{7,199},{8... | collective-permute-start | bytes 196616 | tf_op jit(solution)/shard_map/cols/ppermute | solution.py:56
  31.9 11.3 %collective-permute-start.25 = (f32[128,128]{1,0:T(8,128)S(1)}, f32[128,128]{1,0:T(8,128)S(1)}, u32[]{:S(2)}, u32[]{:S(2)}) collective-permute-start(f32[128,128]{1,0:T(8,128)S(1)} %select_select_fusion.own_ref), channel_id=1, source_target_pairs={{0,9},{1,8},{2,11},{3,10},{4,13},{5,12},{6,15},{7,14},{8,1},{9,0},... | collective-permute-start | bytes 196616 | tf_op jit(solution)/shard_map/diag/ppermute | solution.py:56
  34.9 9.4 %collective-permute-start.23 = (f32[128,128]{1,0:T(8,128)S(1)}, f32[128,128]{1,0:T(8,128)S(1)}, u32[]{:S(2)}, u32[]{:S(2)}) collective-permute-start(f32[128,128]{1,0:T(8,128)S(1)} %select_select_fusion.own_ref), channel_id=1, source_target_pairs={{0,1},{1,0},{2,3},{3,2},{4,5},{5,4},{6,7},{7,6},{8,9},{9,8},{10,11... | collective-permute-start | bytes 196616 | tf_op jit(solution)/shard_map/diag/ppermute | solution.py:56
  35.3 10.2 %collective-permute-start.24 = (f32[128,128]{1,0:T(8,128)S(1)}, f32[128,128]{1,0:T(8,128)S(1)}, u32[]{:S(2)}, u32[]{:S(2)}) collective-permute-start(f32[128,128]{1,0:T(8,128)S(1)} %select_select_fusion.own_ref), channel_id=1, source_target_pairs={{0,8},{1,9},{2,10},{3,11},{4,12},{5,13},{6,14},{7,15},{8,0},{9,1},... | collective-permute-start | bytes 196616 | tf_op jit(solution)/shard_map/diag/ppermute | solution.py:56
  37.7 16.0 %collective-permute-start.22 = (f32[512,128]{1,0:T(8,128)S(1)}, f32[512,128]{1,0:T(8,128)S(1)}, u32[]{:S(2)}, u32[]{:S(2)}) collective-permute-start(f32[512,128]{1,0:T(8,128)S(1)} %pad_maximum_fusion.mine_ref), channel_id=1, source_target_pairs={{0,16},{1,17},{2,18},{3,19},{4,20},{5,21},{6,22},{7,23},{8,24},{9,... | collective-permute-start | bytes 786440 | tf_op jit(solution)/shard_map/cols/ppermute | solution.py:56
  38.5 15.2 %collective-permute-start.21 = (f32[512,128]{1,0:T(8,128)S(1)}, f32[512,128]{1,0:T(8,128)S(1)}, u32[]{:S(2)}, u32[]{:S(2)}) collective-permute-start(f32[512,128]{1,0:T(8,128)S(1)} %pad_maximum_fusion.mine_ref), channel_id=1, source_target_pairs={{0,48},{1,49},{2,50},{3,51},{4,52},{5,53},{6,54},{7,55},{8,56},{9,... | collective-permute-start | bytes 786440 | tf_op jit(solution)/shard_map/cols/ppermute | solution.py:56
  43.2 12.2 %collective-permute-start.20 = (f32[512,128]{1,0:T(8,128)S(1)}, f32[512,128]{1,0:T(8,128)S(1)}, u32[]{:S(2)}, u32[]{:S(2)}) collective-permute-start(f32[512,128]{1,0:T(8,128)S(1)} %pad_maximum_fusion.mine_ref), channel_id=1, source_target_pairs={{0,8},{1,9},{2,10},{3,11},{4,12},{5,13},{6,14},{7,15},{8,0},{9,1},... | collective-permute-start | bytes 786440 | tf_op jit(solution)/shard_map/cols/ppermute | solution.py:56
  44.3 12.2 %collective-permute-start.7 = (f32[512,128]{1,0:T(8,128)S(1)}, f32[512,128]{1,0:T(8,128)S(1)}, u32[]{:S(2)}, u32[]{:S(2)}) collective-permute-start(f32[512,128]{1,0:T(8,128)S(1)} %pad_maximum_fusion.mine_ref), channel_id=1, source_target_pairs={{0,32},{1,33},{2,34},{3,35},{4,36},{5,37},{6,38},{7,39},{8,40},{9,... | collective-permute-start | bytes 786440 | tf_op jit(solution)/shard_map/cols/ppermute | solution.py:56
  45.4 9.9 %collective-permute-start.19 = (f32[512,128]{1,0:T(8,128)S(1)}, f32[512,128]{1,0:T(8,128)S(1)}, u32[]{:S(2)}, u32[]{:S(2)}) collective-permute-start(f32[512,128]{1,0:T(8,128)S(1)} %broadcast_select_fusion.1.near_ref), channel_id=1, source_target_pairs={{0,1},{1,0},{2,3},{3,2},{4,5},{5,4},{6,7},{7,6},{8,9},{9,8},{10,11... | collective-permute-start | bytes 786440 | tf_op jit(solution)/shard_map/diag/ppermute | solution.py:56
  53.7 4.8 %copy-start.1 = (f32[4,1,128,16,1,128]{5,4,3,2,1,0:T(1,128)S(1)}, f32[4,1,128,16,1,128]{5,4,3,2,1,0:T(1,128)}, u32[]{:S(2)}) copy-start(f32[4,1,128,16,1,128]{5,4,3,2,1,0:T(1,128)} %param.1) | copy-start | bytes 12582916
  53.7 3.6 %collective-permute-start.26 = (f32[512,128]{1,0:T(8,128)S(1)}, f32[512,128]{1,0:T(8,128)S(1)}, u32[]{:S(2)}, u32[]{:S(2)}) collective-permute-start(f32[512,128]{1,0:T(8,128)S(1)} %collective-permute-done.21.up_ref), channel_id=1, source_target_pairs={{0,8},{1,9},{2,10},{3,11},{4,12},{5,13},{6,14},{7,15},{8,0},{9,1},... | collective-permute-start | bytes 786440 | tf_op jit(solution)/shard_map/cols/ppermute | solution.py:56
  55.3 2.0 %collective-permute-start.27 = (f32[512,128]{1,0:T(8,128)S(1)}, f32[512,128]{1,0:T(8,128)S(1)}, u32[]{:S(2)}, u32[]{:S(2)}) collective-permute-start(f32[512,128]{1,0:T(8,128)S(1)} %collective-permute-done.22.down_ref), channel_id=1, source_target_pairs={{0,8},{1,9},{2,10},{3,11},{4,12},{5,13},{6,14},{7,15},{8,0},{9,1},... | collective-permute-start | bytes 786440 | tf_op jit(solution)/shard_map/cols/ppermute | solution.py:56
  56.5 2.0 %collective-permute-start.28 = (f32[512,128]{1,0:T(8,128)S(1)}, f32[512,128]{1,0:T(8,128)S(1)}, u32[]{:S(2)}, u32[]{:S(2)}) collective-permute-start(f32[512,128]{1,0:T(8,128)S(1)} %collective-permute-done.7.refs_4_), channel_id=1, source_target_pairs={{0,8},{1,9},{2,10},{3,11},{4,12},{5,13},{6,14},{7,15},{8,0},{9,1},... | collective-permute-start | bytes 786440 | tf_op jit(solution)/shard_map/cols/ppermute | solution.py:56
